TPU v7x, 32 devices: a whole 2x2x4 slice. The times are simulated.
32 devices in a mesh: step: 2 (over x), frame: 4 (over y, core), strip: 4 (over z).
Axes of the slice: x: 2, y: 2, z: 4, core: 2. Of those that a mesh axis runs over, the one named last changes fastest.
Arguments:
- enc_feats: bfloat16 [320, 8, 32, 128], P('step', 'frame', 'strip'), may hold values from -64 to 64
- skip_feats: bfloat16 [320, 8, 32, 128], P('step', 'frame', 'strip'), may hold values from -64 to 64
- timesteps: int32 [2], P('step'), may hold values from 0 to 999
- time_first: bfloat16 [320, 1280], replicated, may hold values from -0.3125 to 0.3125
- time_second: bfloat16 [1280, 1280], replicated, may hold values from -0.15625 to 0.15625
- embed_proj: bfloat16 [1280, 320], replicated, may hold values from -0.15625 to 0.15625
- conv_first: bfloat16 [3, 3, 320, 640], replicated, may hold values from -0.078125 to 0.078125
- conv_second: bfloat16 [3, 3, 320, 320], replicated, may hold values from -0.109375 to 0.109375
- temporal_weight: bfloat16 [3, 320, 320], replicated, may hold values from -0.1875 to 0.1875
- skip_weight: bfloat16 [320, 640], replicated, may hold values from -0.25 to 0.25
Outputs:
- decoded: bfloat16 [2, 320, 8, 32, 128], P('step', None, 'frame', 'strip')
All inputs are finite; a program needn't handle non-finite values.
Results may differ from a plain program's by a relative error of at most 0.0035.
Values may be sent and summed in bfloat16 or wider, within the bound.
A program may use at most 64 MiB of HBM per device.

v0:
```python
import math

import jax
import jax.numpy as jnp
from jax import lax
from jax.sharding import PartitionSpec as P

GROUPS = 32


norm_eps = 1e-05


def with_halo(cells, sides, width):
    for axis, dim in sides:
        count = lax.axis_size(axis)
        ends = count - 1
        head = lax.slice_in_dim(cells, 0, width, axis=dim)
        tail = lax.slice_in_dim(cells, cells.shape[dim] - width, cells.shape[dim], axis=dim)
        cells = jnp.concatenate(
            [
                lax.ppermute(tail, axis, [(i, (i + 1) % count) for i in range(ends)]),
                cells,
                lax.ppermute(head, axis, [((i + 1) % count, i) for i in range(ends)]),
            ],
            axis=dim,
        )
    return cells


def conv_taps(padded, weights):
    row_count = padded.shape[2] - 2
    col_count = padded.shape[3]
    padded_cols = jnp.pad(padded, ((0, 0), (0, 0), (0, 0), (1, 1)))
    running = jnp.zeros((weights.shape[2], padded.shape[1], row_count, col_count), jnp.float32)
    for row_off in range(3):
        for col_off in range(3):
            window = padded_cols[:, :, row_off : row_off + row_count, col_off : col_off + col_count]
            running = running + jnp.einsum(
                "oi,ifhw->ofhw",
                weights[row_off, col_off],
                window,
                preferred_element_type=jnp.float32,
            )
    return running


def channel_scales(sum_one, sum_two, groups, count_all):
    per_group = sum_one.shape[0] // groups
    mean_group = sum_one.reshape(groups, per_group).sum(axis=1) / count_all
    square_group = sum_two.reshape(groups, per_group).sum(axis=1) / count_all
    rstd_group = lax.rsqrt(square_group - mean_group * mean_group + norm_eps)
    return (jnp.repeat(mean_group, per_group), jnp.repeat(rstd_group, per_group))


def on_device(
    enc_feats,
    skip_feats,
    timesteps,
    time_first,
    time_second,
    embed_proj,
    conv_first,
    conv_second,
    temporal_weight,
    skip_weight,
):
    channels = conv_second.shape[2]
    own_chans = enc_feats.shape[0]
    frames = enc_feats.shape[1]
    row_count = enc_feats.shape[2]
    col_count = enc_feats.shape[3]
    spread = lax.axis_size("frame") * lax.axis_size("strip")
    chan_start = lax.axis_index("step") * own_chans
    stacked = jnp.stack([enc_feats, skip_feats])
    wide_feats = stacked.astype(jnp.float32)
    local_one = jnp.sum(wide_feats, axis=(2, 3, 4))
    local_two = jnp.sum(wide_feats * wide_feats, axis=(2, 3, 4))
    anchor = jnp.zeros((), jnp.int32)
    place_one = lax.dynamic_update_slice(
        jnp.zeros((2, channels), jnp.float32), local_one, (anchor, chan_start)
    )
    place_two = lax.dynamic_update_slice(
        jnp.zeros((2, channels), jnp.float32), local_two, (anchor, chan_start)
    )
    total_one, total_two = lax.psum((place_one, place_two), ("step", "frame", "strip"))
    in_count = frames * row_count * col_count * spread * (2 * channels // GROUPS)
    mean_in, rstd_in = channel_scales(
        total_one.reshape(-1), total_two.reshape(-1), GROUPS, in_count
    )
    rimmed = with_halo(stacked, (("strip", 3),), 1)
    strip_at = lax.axis_index("strip")
    strip_last = lax.axis_size("strip") - 1
    positions = jnp.arange(row_count + 2)
    row_keep = (
        ((positions > 0) | (strip_at > 0)) & ((positions < row_count + 1) | (strip_at < strip_last))
    ).astype(jnp.float32)
    pieces = lax.all_gather(rimmed, "step", axis=1, tiled=True)
    chans_here = pieces.shape[1]
    mean_rows = jnp.stack(
        [
            lax.slice_in_dim(mean_in, 0, chans_here, axis=0),
            lax.dynamic_slice_in_dim(mean_in, channels, chans_here),
        ]
    )
    rstd_rows = jnp.stack(
        [
            lax.slice_in_dim(rstd_in, 0, chans_here, axis=0),
            lax.dynamic_slice_in_dim(rstd_in, channels, chans_here),
        ]
    )
    normed = jax.nn.silu(
        (pieces.astype(jnp.float32) - mean_rows[:, :, None, None, None])
        * rstd_rows[:, :, None, None, None]
    )
    normed = normed * row_keep[None, None, None, :, None]
    act_rows = normed.astype(jnp.bfloat16).reshape(2 * chans_here, frames, row_count + 2, col_count)
    tap_weights = jnp.concatenate(
        [
            lax.slice_in_dim(conv_first, 0, chans_here, axis=3),
            lax.dynamic_slice_in_dim(conv_first, channels, chans_here, 3),
        ],
        axis=3,
    )
    skip_cols = jnp.concatenate(
        [
            lax.slice_in_dim(skip_weight, 0, chans_here, axis=1),
            lax.dynamic_slice_in_dim(skip_weight, channels, chans_here, 1),
        ],
        axis=1,
    )
    inner_rows = pieces[:, :, :, 1 : row_count + 1].reshape(
        2 * chans_here, frames, row_count, col_count
    )
    conv_part = conv_taps(act_rows, tap_weights)
    skip_part = jnp.einsum(
        "oi,ifhw->ofhw", skip_cols, inner_rows, preferred_element_type=jnp.float32
    )
    half_chans = channels // 2
    freq_table = jnp.exp(
        -math.log(10000.0) * jnp.arange(half_chans, dtype=jnp.float32) / half_chans
    )
    angle_rows = timesteps.astype(jnp.float32)[:, None] * freq_table[None, :]
    sinus_rows = jnp.concatenate([jnp.cos(angle_rows), jnp.sin(angle_rows)], axis=1).astype(
        jnp.bfloat16
    )
    embed_one = jax.nn.silu(
        jnp.dot(sinus_rows, time_first, preferred_element_type=jnp.float32)
    ).astype(jnp.bfloat16)
    embed_two = jax.nn.silu(
        jnp.dot(embed_one, time_second, preferred_element_type=jnp.float32)
    ).astype(jnp.bfloat16)
    step_embed = jnp.dot(embed_two, embed_proj, preferred_element_type=jnp.float32)
    hidden = conv_part + step_embed[0][:, None, None, None]
    hidden_one = jnp.sum(hidden, axis=(1, 2, 3))
    hidden_two = jnp.sum(hidden * hidden, axis=(1, 2, 3))
    total_hone, total_htwo = lax.psum((hidden_one, hidden_two), ("frame", "strip"))
    mid_count = frames * row_count * col_count * spread * (channels // GROUPS)
    mean_mid, rstd_mid = channel_scales(total_hone, total_htwo, GROUPS, mid_count)
    mid_act = jax.nn.silu(
        (hidden - mean_mid[:, None, None, None]) * rstd_mid[:, None, None, None]
    ).astype(jnp.bfloat16)
    mid_rim = with_halo(mid_act, (("strip", 2),), 1)
    second = conv_taps(mid_rim, conv_second)
    temporal_in = jax.nn.silu(second).astype(jnp.bfloat16)
    framed = with_halo(temporal_in, (("frame", 1),), 1)
    mixed_out = second
    for offset in range(3):
        mixed_out = mixed_out + jnp.einsum(
            "oi,ifhw->ofhw",
            temporal_weight[offset],
            framed[:, offset : offset + frames],
            preferred_element_type=jnp.float32,
        )
    decoded = (skip_part + mixed_out).astype(jnp.bfloat16)
    return decoded[None]


def solution(mesh):
    return jax.shard_map(
        on_device,
        mesh=mesh,
        in_specs=(
            P("step", "frame", "strip", None),
            P("step", "frame", "strip", None),
            P("step"),
            P(),
            P(),
            P(),
            P(),
            P(),
            P(),
            P(),
        ),
        out_specs=P("step", None, "frame", "strip", None),
        check_vma=False,
    )
```

profile of v0, /device:TPU:1, one launch (start us, length us, event | category | flops | bytes accessed | tf_op | source)
XLA Modules:
  0.0 203.4 jit_solution(14955595743087807861)
XLA Ops:
  6.5 1.8 copy_bitcast_fusion
  8.4 4.0 %collective-permute-start = (bf16[2,160,2,1,128]{4,1,3,2,0:T(8,128)(2,1)S(1)}, bf16[2,160,2,1,128]{4,1,3,2,0:T(8,128)(2,1)S(1)}, u32[]{:S(2)}, u32[]{:S(2)}) collective-permute-start(bf16[2,160,2,1,128]{4,1,3,2,0:T(8,128)(2,1)S(1)} %get-tuple-element.17), channel_id=1, source_target_pairs={{0,1},{1,2},{2,3},{4,5},{5,6},{6,7},{8,9},{9,10},{10,11},{12,13},{... | collective-permute-start | bytes 491528 | tf_op jit(solution)/shard_map/ppermute | solution.py:22
  13.7 1.5 collective-permute-done
  15.3 3.8 %collective-permute-done.1 = bf16[2,160,2,1,128]{4,1,3,2,0:T(8,128)(2,1)S(1)} collective-permute-done((bf16[2,160,2,1,128]{4,1,3,2,0:T(8,128)(2,1)S(1)}, bf16[2,160,2,1,128]{4,1,3,2,0:T(8,128)(2,1)S(1)}, u32[]{:S(2)}, u32[]{:S(2)}) %collective-permute-start.1) | collective-permute-done | bytes 163872 | tf_op jit(solution)/shard_map/ppermute | solution.py:24
  19.1 1.4 pad_maximum_fusion.1
  21.3 1.4 convolution_reduce_fusion.1
  23.3 1.8 convert_reduce_fusion
  25.6 42.8 %all-reduce.2 = (f32[32,20]{1,0:T(8,128)S(1)}, f32[32,20]{1,0:T(8,128)S(1)}) all-reduce(f32[32,20]{1,0:T(8,128)S(1)} %reshape_reshape.7, f32[32,20]{1,0:T(8,128)S(1)} %reshape_reshape.6), channel_id=1, replica_groups=mesh['step'=2,'frame'=4,'strip'=4] {'step','frame','strip'}, use_global_device_ids=true, to_apply=%region_4.0 | all-reduce | flops 1280 | bytes 10240 | tf_op jit(solution)/shard_map/psum | solution.py:86
  69.5 1.5 convolution_reduce_fusion.2
  71.0 4.1 %multiply_convert_fusion = bf16[2,320,2,10,128]{4,1,3,2,0:T(8,128)(2,1)S(1)} fusion(bf16[2,320,2,10,128]{4,1,3,2,0:T(8,128)(2,1)} %all-gather.2.cloned.1.call-done, f32[10]{0:T(128)S(1)} %and_convert_fusion, f32[2,320]{1,0:T(2,128)S(1)} %pad_maximum_fusion.11, f32[2,320]{1,0:T(2,128)S(1)} %pad_maximum_fusion.10), kind=kLoop, calls=%fused_computation.8 | loop fusion | flops 14745600 | bytes 6558760 | tf_op jit(solution)/shard_map/convert_element_type | solution.py:117
  75.4 1.8 copy-done.6
  77.2 1.4 fusion.8
  78.6 1.4 fusion.9
  79.9 1.4 fusion.10
  81.3 1.4 fusion.11
  82.7 1.4 fusion.12
  86.4 1.4 fusion.7
  87.8 4.7 %fusion.112 = (f32[320]{0:T(512)S(1)}, f32[320]{0:T(512)S(1)}, f32[2,8,128,320]{2,3,1,0:T(8,128)}) fusion(f32[320]{0:T(512)S(1)} %convolution_reduce_fusion.2, f32[2,8,128,320]{2,3,1,0:T(8,128)S(1)} %fusion.12, f32[2,8,128,320]{2,3,1,0:T(8,128)S(1)} %fusion.13, f32[2,8,128,320]{2,3,1,0:T(8,128)S(1)} %fusion.11, f32[2,8,128,320]{2,3,1,0:T(8,128)S(1)} %fusion.10, ...), kind=kOutput, calls=%fused_computation.157 | convolution fusion | flops 846724480 | bytes 26628608 | tf_op jit(solution)/shard_map/oi,ifhw->ofhw/dot_general | solution.py:39
  92.7 57.3 %all-reduce.3 = (f32[32,10]{1,0:T(8,128)S(1)}, f32[32,10]{1,0:T(8,128)S(1)}) all-reduce(f32[32,10]{1,0:T(8,128)S(1)} %reshape.78, f32[32,10]{1,0:T(8,128)S(1)} %reshape.77), channel_id=1, replica_groups=mesh['step'=2,'frame'=4,'strip'=4] {'frame','strip'}, use_global_device_ids=true, to_apply=%region_10.11 | all-reduce | flops 640 | bytes 5120 | tf_op jit(solution)/shard_map/psum | solution.py:157
  150.6 2.6 %fusion.30 = bf16[320,2,8,128]{3,0,2,1:T(8,128)(2,1)S(1)} fusion(f32[2,8,128,320]{2,3,1,0:T(8,128)} %get-tuple-element.27, f32[320]{0:T(512)S(1)} %mul.97, f32[320]{0:T(512)S(1)} %sub.27), kind=kLoop, calls=%fused_computation.51 | loop fusion | flops 4587520 | bytes 3934720 | tf_op jit(solution)/shard_map/convert_element_type | solution.py:162
  153.3 1.3 collective-permute-start.2
  155.9 1.8 fusion.82
  157.7 1.7 slice-done
  159.4 1.7 copy.22
  161.2 2.3 %fusion.5 = bf16[320,2,10,130]{3,0,2,1:T(8,128)(2,1)S(1)} fusion(bf16[320,2,1,128]{3,0,2,1:T(8,128)(2,1)S(1)} %collective-permute-done.3, bf16[320,2,8,128]{3,0,2,1:T(8,128)(2,1)S(1)} %fusion.30, bf16[320,2,1,128]{3,0,2,1:T(8,128)(2,1)S(1)} %collective-permute-done.2), kind=kLoop, calls=%fused_computation.14 | loop fusion | flops 9984000 | bytes 3302400 | tf_op jit(solution)/shard_map/concatenate | solution.py:20
  166.1 2.5 %fusion.49 = f32[2,8,128,320]{2,3,1,0:T(8,128)} fusion(bf16[320,2,10,130]{3,0,2,1:T(8,128)(2,1)S(1)} %fusion.5, bf16[3,3,320,320]{3,2,1,0:T(8,128)(2,1)S(1)} %copy-done.4), kind=kOutput, calls=%fused_computation.75 | convolution fusion | flops 419430400 | bytes 4177920 | tf_op jit(solution)/shard_map/oi,ifhw->ofhw/dot_general | solution.py:39
  168.6 2.4 %fusion.53 = f32[2,8,128,320]{2,3,1,0:T(8,128)} fusion(bf16[320,2,10,130]{3,0,2,1:T(8,128)(2,1)S(1)} %fusion.5, bf16[3,3,320,320]{3,2,1,0:T(8,128)(2,1)S(1)} %copy-done.4), kind=kOutput, calls=%fused_computation.80 | convolution fusion | flops 419430400 | bytes 4177920 | tf_op jit(solution)/shard_map/oi,ifhw->ofhw/dot_general | solution.py:39
  172.6 3.9 %fusion.29 = (bf16[320,2,8,128]{3,0,2,1:T(8,128)(2,1)S(1)}, f32[2,8,128,320]{2,3,1,0:T(8,128)S(1)}) fusion(bf16[320,2,10,130]{3,0,2,1:T(8,128)(2,1)S(1)} %fusion.5, bf16[3,3,320,320]{3,2,1,0:T(8,128)(2,1)} %param.17, f32[2,8,128,320]{2,3,1,0:T(8,128)S(1)} %fusion.41, f32[2,8,128,320]{2,3,1,0:T(8,128)S(1)} %fusion.43, f32[2,8,128,320]{2,3,1,0:T(8,128)S(1)} %fusion.45, ...), kind=kOutput, calls=%fused_computation.50 | convolution fusion | flops 427950080 | bytes 26460160 | tf_op jit(solution)/shard_map/oi,ifhw->ofhw/dot_general | solution.py:39
  176.7 6.2 %collective-permute-start.5 = (bf16[320,1,8,128]{3,0,2,1:T(8,128)(2,1)S(1)}, bf16[320,1,8,128]{3,0,2,1:T(8,128)(2,1)S(1)}, u32[]{:S(2)}, u32[]{:S(2)}) collective-permute-start(bf16[320,1,8,128]{3,0,2,1:T(8,128)(2,1)S(1)} %get-tuple-element.13), channel_id=1, source_target_pairs={{4,0},{8,4},{12,8},{5,1},{9,5},{13,9},{6,2},{10,6},{14,10},{7,3},{... | collective-permute-start | bytes 1966088 | tf_op jit(solution)/shard_map/ppermute | solution.py:24
  182.9 2.4 %collective-permute-start.4 = (bf16[320,1,8,128]{3,0,2,1:T(8,128)(2,1)S(1)}, bf16[320,1,8,128]{3,0,2,1:T(8,128)(2,1)S(1)}, u32[]{:S(2)}, u32[]{:S(2)}) collective-permute-start(bf16[320,1,8,128]{3,0,2,1:T(8,128)(2,1)S(1)} %get-tuple-element.14), channel_id=1, source_target_pairs={{0,4},{4,8},{8,12},{1,5},{5,9},{9,13},{2,6},{6,10},{10,14},{3,7},{... | collective-permute-start | bytes 1966088 | tf_op jit(solution)/shard_map/ppermute | solution.py:22
  187.4 5.4 %collective-permute-done.4 = bf16[320,1,8,128]{3,0,2,1:T(8,128)(2,1)S(1)} collective-permute-done((bf16[320,1,8,128]{3,0,2,1:T(8,128)(2,1)S(1)}, bf16[320,1,8,128]{3,0,2,1:T(8,128)(2,1)S(1)}, u32[]{:S(2)}, u32[]{:S(2)}) %collective-permute-start.4) | collective-permute-done | bytes 655392 | tf_op jit(solution)/shard_map/ppermute | solution.py:22
  194.7 1.9 copy.25
  (78 shorter events, 16.7 us)
Async XLA Ops:
  6.5 16.2 %copy-start = (bf16[1280,1280]{1,0:T(8,128)(2,1)S(1)}, bf16[1280,1280]{1,0:T(8,128)(2,1)}, u32[]{:S(2)}) copy-start(bf16[1280,1280]{1,0:T(8,128)(2,1)} %param.14) | copy-start | bytes 9830404
  6.5 64.5 %all-gather.2.cloned.1.call-start = ((), (), s32[]{:S(2)}) async-start(), calls=%async_computation | async-start | bytes 4915200 | tf_op jit(solution)/shard_map/all_gather | solution.py:98
  8.3 10.8 %copy-start.2 = (bf16[1,160,2,8,128]{4,1,3,2,0:T(8,128)(2,1)}, bf16[1,160,2,8,128]{4,1,3,2,0:T(8,128)(2,1)S(1)}, u32[]{:S(2)}) copy-start(bf16[1,160,2,8,128]{4,1,3,2,0:T(8,128)(2,1)S(1)} %get-tuple-element.30) | copy-start | bytes 1966084
  8.3 10.7 %copy-start.3 = (bf16[1,160,2,8,128]{4,1,3,2,0:T(8,128)(2,1)}, bf16[1,160,2,8,128]{4,1,3,2,0:T(8,128)(2,1)S(1)}, u32[]{:S(2)}) copy-start(bf16[1,160,2,8,128]{4,1,3,2,0:T(8,128)(2,1)S(1)} %get-tuple-element.31) | copy-start | bytes 1966084
  8.4 6.9 %collective-permute-start = (bf16[2,160,2,1,128]{4,1,3,2,0:T(8,128)(2,1)S(1)}, bf16[2,160,2,1,128]{4,1,3,2,0:T(8,128)(2,1)S(1)}, u32[]{:S(2)}, u32[]{:S(2)}) collective-permute-start(bf16[2,160,2,1,128]{4,1,3,2,0:T(8,128)(2,1)S(1)} %get-tuple-element.17), channel_id=1, source_target_pairs={{0,1},{1,2},{2,3},{4,5},{5,6},{6,7},{8,9},{9,10},{10,11},{12,13},{... | collective-permute-start | bytes 491528 | tf_op jit(solution)/shard_map/ppermute | solution.py:22
  12.4 6.6 %collective-permute-start.1 = (bf16[2,160,2,1,128]{4,1,3,2,0:T(8,128)(2,1)S(1)}, bf16[2,160,2,1,128]{4,1,3,2,0:T(8,128)(2,1)S(1)}, u32[]{:S(2)}, u32[]{:S(2)}) collective-permute-start(bf16[2,160,2,1,128]{4,1,3,2,0:T(8,128)(2,1)S(1)} %get-tuple-element.18), channel_id=1, source_target_pairs={{1,0},{2,1},{3,2},{5,4},{6,5},{7,6},{9,8},{10,9},{11,10},{13,12},{... | collective-permute-start | bytes 491528 | tf_op jit(solution)/shard_map/ppermute | solution.py:24
  75.2 2.0 %copy-start.6 = (bf16[3,3,320,640]{3,2,1,0:T(8,128)(2,1)S(1)}, bf16[3,3,320,640]{3,2,1,0:T(8,128)(2,1)}, u32[]{:S(2)}) copy-start(bf16[3,3,320,640]{3,2,1,0:T(8,128)(2,1)} %param.16) | copy-start | bytes 11059204
  153.3 7.9 %collective-permute-start.2 = (bf16[320,2,1,128]{3,0,2,1:T(8,128)(2,1)S(1)}, bf16[320,2,1,128]{3,0,2,1:T(8,128)(2,1)S(1)}, u32[]{:S(2)}, u32[]{:S(2)}) collective-permute-start(bf16[320,2,1,128]{3,0,2,1:T(8,128)(2,1)S(1)} %get-tuple-element.15), channel_id=1, source_target_pairs={{0,1},{1,2},{2,3},{4,5},{5,6},{6,7},{8,9},{9,10},{10,11},{12,13},{... | collective-permute-start | bytes 491528 | tf_op jit(solution)/shard_map/ppermute | solution.py:22
  154.6 6.6 %collective-permute-start.3 = (bf16[320,2,1,128]{3,0,2,1:T(8,128)(2,1)S(1)}, bf16[320,2,1,128]{3,0,2,1:T(8,128)(2,1)S(1)}, u32[]{:S(2)}, u32[]{:S(2)}) collective-permute-start(bf16[320,2,1,128]{3,0,2,1:T(8,128)(2,1)S(1)} %get-tuple-element.16), channel_id=1, source_target_pairs={{1,0},{2,1},{3,2},{5,4},{6,5},{7,6},{9,8},{10,9},{11,10},{13,12},{... | collective-permute-start | bytes 491528 | tf_op jit(solution)/shard_map/ppermute | solution.py:24
  157.7 1.7 slice-start
  161.1 2.3 %copy-start.4 = (bf16[3,3,320,320]{3,2,1,0:T(8,128)(2,1)S(1)}, bf16[3,3,320,320]{3,2,1,0:T(8,128)(2,1)}, u32[]{:S(2)}) copy-start(bf16[3,3,320,320]{3,2,1,0:T(8,128)(2,1)} %param.17) | copy-start | bytes 5529604
  176.6 8.8 %copy-start.7 = (bf16[320,640]{1,0:T(8,128)(2,1)S(1)}, bf16[320,640]{1,0:T(8,128)(2,1)}, u32[]{:S(2)}) copy-start(bf16[320,640]{1,0:T(8,128)(2,1)} %param.19) | copy-start | bytes 1228804
  176.7 17.0 %collective-permute-start.5 = (bf16[320,1,8,128]{3,0,2,1:T(8,128)(2,1)S(1)}, bf16[320,1,8,128]{3,0,2,1:T(8,128)(2,1)S(1)}, u32[]{:S(2)}, u32[]{:S(2)}) collective-permute-start(bf16[320,1,8,128]{3,0,2,1:T(8,128)(2,1)S(1)} %get-tuple-element.13), channel_id=1, source_target_pairs={{4,0},{8,4},{12,8},{5,1},{9,5},{13,9},{6,2},{10,6},{14,10},{7,3},{... | collective-permute-start | bytes 1966088 | tf_op jit(solution)/shard_map/ppermute | solution.py:24
  182.9 9.9 %collective-permute-start.4 = (bf16[320,1,8,128]{3,0,2,1:T(8,128)(2,1)S(1)}, bf16[320,1,8,128]{3,0,2,1:T(8,128)(2,1)S(1)}, u32[]{:S(2)}, u32[]{:S(2)}) collective-permute-start(bf16[320,1,8,128]{3,0,2,1:T(8,128)(2,1)S(1)} %get-tuple-element.14), channel_id=1, source_target_pairs={{0,4},{4,8},{8,12},{1,5},{5,9},{9,13},{2,6},{6,10},{10,14},{3,7},{... | collective-permute-start | bytes 1966088 | tf_op jit(solution)/shard_map/ppermute | solution.py:22
  185.3 1.2 copy-start.5
  193.7 2.9 %copy-start.1 = (bf16[1280,1280]{1,0:T(8,128)(2,1)S(1)}, bf16[1280,1280]{1,0:T(8,128)(2,1)}, u32[]{:S(2)}) copy-start(bf16[1280,1280]{1,0:T(8,128)(2,1)} %param.14) | copy-start | bytes 9830404
Sparse Core Ops, SparseCore 0:
  20.6 49.2 all-gather.1
where the time goes:
time: 204 us; the launch traced here: 203 us
  blocking collectives  100 us (49%)
  matrix products  37.4 us (18%)
  starting transfers between devices  16.6 us (8%)
  between operations  14.6 us (7%)
  other arithmetic  12.8 us (6%)
  local copies, waits for them, and re-layouts  11.2 us (5%)
  waiting for transfers between devices  10.8 us (5%)
    psum x1, blocking collectives, on_device(): lax.psum((hidden_one, hidden_two), ('frame', 'strip'))  57.3 us
    psum x1, blocking collectives, on_device(): lax.psum((place_one, place_two), ('step', 'frame', 'strip'))  42.8 us
    dot_general x18, matrix products, conv_taps(): jnp.einsum('oi,ifhw->ofhw', weights[row_off, col_off], window, preferred_...  30.2 us
    ppermute x3, starting transfers between devices, with_halo(): lax.ppermute(head, axis, [((i + 1) % count, i) for i in range(ends)])  8.79 us
    ppermute x3, starting transfers between devices, with_halo(): lax.ppermute(tail, axis, [(i, (i + 1) % count) for i in range(ends)])  7.76 us
    ppermute x3, waiting for transfers between devices, with_halo(): lax.ppermute(tail, axis, [(i, (i + 1) % count) for i in range(ends)])  6.98 us
    convert_element_type x1, other arithmetic, on_device(): normed.astype(jnp.bfloat16)  4.1 us
  transfers between devices with their start and end apart: 7, of which 3 were waited for; matrix products, arithmetic and copies ran while one was open for 7% of the time, Pallas kernels for 0%

commit v1 on v0

--- a/solution.py
+++ b/solution.py
@@ -1,8 +1,11 @@
+import functools
 import math
 
 import jax
 import jax.numpy as jnp
 from jax import lax
+from jax.experimental import pallas as pl
+from jax.experimental.pallas import tpu as pltpu
 from jax.sharding import PartitionSpec as P
 
 GROUPS = 32
@@ -176,9 +179,515 @@
     return decoded[None]
 
 
+MESH = pl.DeviceIdType.MESH
+HIGH = lax.Precision.HIGHEST
+
+
+def silu(v):
+    h = 0.5 * v
+    return h + h * jnp.tanh(h)
+
+
+def lane_dot(a, b):
+    return lax.dot_general(
+        a, b, (((1,), (1,)), ((), ())), precision=HIGH, preferred_element_type=jnp.float32
+    )
+
+
+def one_hot(shape, dim, per_group, offset):
+    chan = lax.broadcasted_iota(jnp.int32, shape, dim)
+    group = lax.broadcasted_iota(jnp.int32, shape, 1 - dim) - offset
+    low = group * per_group
+    return jnp.where((chan >= low) & (chan < low + per_group), 1.0, 0.0).astype(jnp.float32)
+
+
+def pack_sums(one, two, per_group):
+    count = one.shape[0]
+    groups = count // per_group
+    tall = jnp.dot(
+        one_hot((128, count), 1, per_group, 0), one, precision=HIGH, preferred_element_type=jnp.float32
+    ) + jnp.dot(
+        one_hot((128, count), 1, per_group, groups), two, precision=HIGH, preferred_element_type=jnp.float32
+    )
+    return lane_dot(jnp.ones((8, 128), jnp.float32), tall)
+
+
+def columns_of(total, count, per_group, entries):
+    groups = count // per_group
+    mean = lane_dot(one_hot((count, 128), 0, per_group, 0), total)[:, :1] / entries
+    square = lane_dot(one_hot((count, 128), 0, per_group, groups), total)[:, :1] / entries
+    rstd = lax.rsqrt(square - mean * mean + norm_eps)
+    return jnp.broadcast_to(mean, (count, 128)), jnp.broadcast_to(rstd, (count, 128))
+
+
+def push(src, dst, send, recv, axis, target):
+    return pltpu.make_async_remote_copy(
+        src_ref=src, dst_ref=dst, send_sem=send, recv_sem=recv,
+        device_id={axis: target}, device_id_type=MESH,
+    )
+
+
+def sum_over(axis, n, src, slots, send, recv):
+    me = lax.axis_index(axis)
+    copies = [
+        push(src, slots.at[d - 1], send.at[d - 1], recv.at[d - 1], axis, lax.rem(me + d, n))
+        for d in range(1, n)
+    ]
+    for copy in copies:
+        copy.start()
+    total = src[...]
+    for d, copy in enumerate(copies):
+        copy.wait_recv()
+        total = total + slots[d]
+    for copy in copies:
+        copy.wait_send()
+    return total
+
+
+def put_taps(value, store):
+    lane = lax.broadcasted_iota(jnp.int32, value.shape, 1)
+    store(0, jnp.where(lane == 0, 0.0, pltpu.roll(value, 1, 1)).astype(jnp.bfloat16))
+    store(1, value.astype(jnp.bfloat16))
+    store(2, jnp.where(lane == 127, 0.0, pltpu.roll(value, 127, 1)).astype(jnp.bfloat16))
+
+
+def block_kernel(
+    sizes,
+    feats, sinus, first_h, second_h, proj_h, conv1_h, conv2_h, temp_h, skip_h,
+    out,
+    raw, act, hid, act2, tbuf, acc1, acc2, cols_in, cols_mid, emb,
+    w1, w2raw, w2, wtraw, wt, ws, tf, ts, ep,
+    stats, slots_strip, slots_frame, slot_step,
+    wsem, own_sem, x_send, x_recv, h_send, h_recv, g_send, g_recv, m_send, m_recv,
+    t_send, t_recv, ss_send, ss_recv, sf_send, sf_recv, sx_send, sx_recv,
+):
+    n_frame, n_strip = sizes
+    rows, own = feats.shape[0], feats.shape[2]
+    chans = 2 * own
+    last = rows - 1
+    step, frame, strip = (lax.axis_index(a) for a in ("step", "frame", "strip"))
+    partner = 1 - step
+    mine = pl.ds(pl.multiple_of(step * own, 16), own)
+    theirs = pl.ds(pl.multiple_of(partner * own, 16), own)
+
+    loads = [
+        pltpu.make_async_copy(conv1_h.at[t // 3, t % 3], w1.at[:, pl.ds(t * 2 * chans, 2 * chans)], wsem.at[t])
+        for t in range(9)
+    ]
+    small = [
+        pltpu.make_async_copy(src, dst, wsem.at[9 + i])
+        for i, (src, dst) in enumerate(
+            ((first_h, tf), (second_h, ts), (proj_h, ep), (conv2_h, w2raw), (temp_h, wtraw), (skip_h, ws))
+        )
+    ]
+    keep = pltpu.make_async_copy(feats, raw.at[pl.ds(1, rows), :, mine, :], own_sem)
+    keep.start()
+
+    barrier = pltpu.get_barrier_semaphore()
+    for axis, n in (("step", 2), ("frame", n_frame), ("strip", n_strip)):
+        for d in range(1, n):
+            pl.semaphore_signal(
+                barrier, inc=1, device_id={axis: lax.rem(lax.axis_index(axis) + d, n)}, device_id_type=MESH
+            )
+    pl.semaphore_wait(barrier, 1 + n_frame - 1 + n_strip - 1)
+
+    def row_copy(r):
+        return push(feats.at[r], raw.at[r + 1, :, mine, :], x_send.at[r], x_recv.at[r], "step", partner)
+
+    def own_up():
+        return push(feats.at[0], raw.at[rows + 1, :, mine, :], h_send.at[1], h_recv.at[1], "strip", strip - 1)
+
+    def own_down():
+        return push(feats.at[last], raw.at[0, :, mine, :], h_send.at[0], h_recv.at[0], "strip", strip + 1)
+
+    def far_up():
+        return push(
+            raw.at[1, :, theirs, :], raw.at[rows + 1, :, theirs, :], g_send.at[1], g_recv.at[1], "strip", strip - 1
+        )
+
+    def far_down():
+        return push(
+            raw.at[rows, :, theirs, :], raw.at[0, :, theirs, :], g_send.at[0], g_recv.at[0], "strip", strip + 1
+        )
+
+    has_up, has_down = strip > 0, strip < n_strip - 1
+    for r in (0, last):
+        row_copy(r).start()
+    pl.when(has_up)(lambda: own_up().start())
+    pl.when(has_down)(lambda: own_down().start())
+
+    @pl.loop(1, last)
+    def _(r):
+        row_copy(r).start()
+
+    for load in loads + small:
+        load.start()
+
+    acc1[...] = jnp.zeros_like(acc1)
+    acc2[...] = jnp.zeros_like(acc2)
+
+    @pl.loop(0, rows)
+    def _(r):
+        for h in range(2):
+            wide = feats[r, h].astype(jnp.float32)
+            a, b = wide[:, :128], wide[:, 128:]
+            at = pl.ds(h * own, own)
+            acc1[at, :] = acc1[at, :] + (a + b)
+            acc2[at, :] = acc2[at, :] + (a * a + b * b)
+
+    per_in = 2 * chans // GROUPS
+    stats[0] = pack_sums(acc1[...], acc2[...], per_in)
+    stats[1] = sum_over("strip", n_strip, stats.at[0], slots_strip.at[0], ss_send.at[0], ss_recv.at[0])
+    stats[2] = sum_over("frame", n_frame, stats.at[1], slots_frame.at[0], sf_send.at[0], sf_recv.at[0])
+    swap = push(stats.at[2], slot_step, sx_send, sx_recv, "step", partner)
+    swap.start()
+    entries = 2 * rows * 128 * n_frame * n_strip
+    in_entries = float(entries * per_in)
+
+    def set_cols(total, at):
+        mean, rstd = columns_of(total, chans, per_in, in_entries)
+        for h in range(2):
+            cols_in[0, h, at, :] = mean[h * own : (h + 1) * own]
+            cols_in[1, h, at, :] = rstd[h * own : (h + 1) * own]
+
+    set_cols(stats[2], mine)
+
+    def make_act(r, at):
+        for h in range(2):
+            mean, rstd = cols_in[0, h, at, :], cols_in[1, h, at, :]
+            for f in range(2):
+                lanes = pl.ds(f * 128, 128)
+                value = silu((raw[r, h, at, lanes].astype(jnp.float32) - mean) * rstd)
+
+                def store(t, v):
+                    act[r, t, h, at, lanes] = v
+
+                put_taps(value, store)
+
+    keep.wait()
+
+    @pl.loop(1, rows + 1)
+    def _(r):
+        make_act(r, mine)
+
+    @pl.when(has_up)
+    def _():
+        own_down().wait_recv()
+        make_act(0, mine)
+
+    @pl.when(has_down)
+    def _():
+        own_up().wait_recv()
+        make_act(rows + 1, mine)
+
+    @pl.when(strip == 0)
+    def _():
+        act[0] = jnp.zeros(act.shape[1:], jnp.bfloat16)
+
+    @pl.when(strip == n_strip - 1)
+    def _():
+        act[rows + 1] = jnp.zeros(act.shape[1:], jnp.bfloat16)
+
+    swap.wait()
+    set_cols(slot_step[...], theirs)
+
+    for load in small:
+        load.wait()
+    one = silu(jnp.dot(sinus[...], tf[...], preferred_element_type=jnp.float32)).astype(jnp.bfloat16)
+    two = silu(jnp.dot(one, ts[...], preferred_element_type=jnp.float32)).astype(jnp.bfloat16)
+    embed = jnp.dot(two, ep[...], preferred_element_type=jnp.float32)
+    emb[...] = jnp.broadcast_to(
+        lane_dot(one_hot((chans, chans), 0, 1, 0), embed[:8])[:, :1], (chans, 128)
+    )
+    for t in range(9):
+        w2[:, t * chans : (t + 1) * chans] = w2raw[t // 3, t % 3]
+    for t in range(3):
+        wt[:, t * chans : (t + 1) * chans] = wtraw[t]
+    for load in loads:
+        load.wait()
+
+    def arrive(r):
+        row_copy(r).wait_recv()
+        make_act(r + 1, theirs)
+
+    arrive(0)
+    pl.when(has_up)(lambda: far_up().start())
+    arrive(last)
+    pl.when(has_down)(lambda: far_down().start())
+    arrive(1)
+    acc1[...] = jnp.zeros_like(acc1)
+    acc2[...] = jnp.zeros_like(acc2)
+
+    @pl.loop(0, rows)
+    def _(i):
+        high = i // 4
+        three = (i // 3) % 2 * (1 - high)
+        c = (i + 1) * (1 - high) * (1 - three) + i * high
+
+        @pl.when((i < 3) | ((i > 3) & (i < rows - 2)))
+        def _():
+            arrive(c + 1)
+
+        @pl.when((i == 3) & has_up)
+        def _():
+            far_down().wait_recv()
+            make_act(0, theirs)
+
+        @pl.when((i == 3) & has_down)
+        def _():
+            far_up().wait_recv()
+            make_act(rows + 1, theirs)
+
+        window = act[pl.ds(c, 3)].reshape(18 * chans, 256)
+        found = jnp.dot(w1[...], window, preferred_element_type=jnp.float32)
+        a, b = found[:, :128] + emb[...], found[:, 128:] + emb[...]
+        hid[c, :, :128] = a
+        hid[c, :, 128:] = b
+        acc1[...] = acc1[...] + (a + b)
+        acc2[...] = acc2[...] + (a * a + b * b)
+
+    per_mid = chans // GROUPS
+    stats[3] = pack_sums(acc1[...], acc2[...], per_mid)
+    stats[4] = sum_over("strip", n_strip, stats.at[3], slots_strip.at[1], ss_send.at[1], ss_recv.at[1])
+    total = sum_over("frame", n_frame, stats.at[4], slots_frame.at[1], sf_send.at[1], sf_recv.at[1])
+    mean, rstd = columns_of(total, chans, per_mid, float(entries * per_mid))
+    cols_mid[0] = mean
+    cols_mid[1] = rstd
+
+    def mid_row(r):
+        for f in range(2):
+            lanes = pl.ds(f * 128, 128)
+            value = silu((hid[r, :, lanes] - cols_mid[0]) * cols_mid[1])
+
+            def store(t, v):
+                act2[r + 1, t, :, lanes] = v
+
+            put_taps(value, store)
+
+    def mid_up():
+        return push(act2.at[1, 1], act2.at[rows + 1, 1], m_send.at[1], m_recv.at[1], "strip", strip - 1)
+
+    def mid_down():
+        return push(act2.at[rows, 1], act2.at[0, 1], m_send.at[0], m_recv.at[0], "strip", strip + 1)
+
+    mid_row(0)
+    pl.when(has_up)(lambda: mid_up().start())
+    mid_row(last)
+    pl.when(has_down)(lambda: mid_down().start())
+
+    @pl.loop(1, last)
+    def _(r):
+        mid_row(r)
+
+    def edge_row(r):
+        for f in range(2):
+            lanes = pl.ds(f * 128, 128)
+            value = act2[r, 1, :, lanes].astype(jnp.float32)
+
+            def store(t, v):
+                if t != 1:
+                    act2[r, t, :, lanes] = v
+
+            put_taps(value, store)
+
+    has_prev, has_next = frame > 0, frame < n_frame - 1
+
+    def to_prev(c):
+        return push(
+            tbuf.at[c, 1, :, pl.ds(0, 128)], tbuf.at[c, 2, :, pl.ds(128, 128)],
+            t_send.at[0, c], t_recv.at[0, c], "frame", frame - 1,
+        )
+
+    def to_next(c):
+        return push(
+            tbuf.at[c, 1, :, pl.ds(128, 128)], tbuf.at[c, 0, :, pl.ds(0, 128)],
+            t_send.at[1, c], t_recv.at[1, c], "frame", frame + 1,
+        )
+
+    def inner_first(i):
+        tail = i // (rows - 2)
+        return (i + 1) * (1 - tail) + (i - (rows - 2)) * last * tail
+
+    @pl.loop(0, rows)
+    def _(i):
+        c = inner_first(i)
+
+        @pl.when((i == rows - 2) & has_up)
+        def _():
+            mid_down().wait_recv()
+            edge_row(0)
+
+        @pl.when((i == rows - 2) & has_down)
+        def _():
+            mid_up().wait_recv()
+            edge_row(rows + 1)
+
+        @pl.when((i == rows - 2) & (strip == 0))
+        def _():
+            act2[0] = jnp.zeros(act2.shape[1:], jnp.bfloat16)
+
+        @pl.when((i == rows - 2) & (strip == n_strip - 1))
+        def _():
+            act2[rows + 1] = jnp.zeros(act2.shape[1:], jnp.bfloat16)
+
+        window = act2[pl.ds(c, 3)].reshape(9 * chans, 256)
+        found = jnp.dot(w2[...], window, preferred_element_type=jnp.float32)
+        hid[c] = found
+        inner = silu(found).astype(jnp.bfloat16)
+        tbuf[c, 1] = inner
+        tbuf[c, 0, :, 128:] = inner[:, :128]
+        tbuf[c, 2, :, :128] = inner[:, 128:]
+
+        @pl.when(has_prev)
+        def _():
+            to_prev(c).start()
+
+        @pl.when(has_next)
+        def _():
+            to_next(c).start()
+
+        @pl.when(frame == 0)
+        def _():
+            tbuf[c, 0, :, :128] = jnp.zeros((chans, 128), jnp.bfloat16)
+
+        @pl.when(frame == n_frame - 1)
+        def _():
+            tbuf[c, 2, :, 128:] = jnp.zeros((chans, 128), jnp.bfloat16)
+
+    @pl.loop(0, rows)
+    def _(i):
+        c = inner_first(i)
+        base = hid[c] + jnp.dot(
+            ws[...], raw[c + 1].reshape(2 * chans, 256), preferred_element_type=jnp.float32
+        )
+
+        @pl.when(has_prev)
+        def _():
+            to_next(c).wait_recv()
+
+        @pl.when(has_next)
+        def _():
+            to_prev(c).wait_recv()
+
+        mixed = jnp.dot(
+            wt[...], tbuf[c].reshape(3 * chans, 256), preferred_element_type=jnp.float32
+        )
+        out[c] = (base + mixed).astype(jnp.bfloat16)
+
+    @pl.loop(0, rows)
+    def _(r):
+        row_copy(r).wait_send()
+
+        @pl.when(has_prev)
+        def _():
+            to_prev(r).wait_send()
+
+        @pl.when(has_next)
+        def _():
+            to_next(r).wait_send()
+
+    @pl.when(has_up)
+    def _():
+        own_up().wait_send()
+        far_up().wait_send()
+        mid_up().wait_send()
+
+    @pl.when(has_down)
+    def _():
+        own_down().wait_send()
+        far_down().wait_send()
+        mid_down().wait_send()
+
+
+def in_kernel(
+    enc_feats, skip_feats, timesteps, time_first, time_second, embed_proj,
+    conv_first, conv_second, temporal_weight, skip_weight,
+):
+    own, frames, rows, cols = enc_feats.shape
+    chans = conv_second.shape[2]
+    width = frames * cols
+    temb = time_first.shape[1]
+    n_frame, n_strip = lax.axis_size("frame"), lax.axis_size("strip")
+    feats = jnp.stack([enc_feats, skip_feats]).transpose(3, 0, 1, 2, 4).reshape(rows, 2, own, width)
+    half_chans = chans // 2
+    freq_table = jnp.exp(
+        -math.log(10000.0) * jnp.arange(half_chans, dtype=jnp.float32) / half_chans
+    )
+    angle_rows = timesteps.astype(jnp.float32)[:, None] * freq_table[None, :]
+    sinus = jnp.concatenate([jnp.cos(angle_rows), jnp.sin(angle_rows)], axis=1).astype(jnp.bfloat16)
+    sinus = jnp.broadcast_to(sinus, (16, chans))
+    bf16, f32 = jnp.bfloat16, jnp.float32
+    dma = pltpu.SemaphoreType.DMA
+    anywhere = pl.BlockSpec(memory_space=pl.ANY)
+    inside = pl.BlockSpec(memory_space=pltpu.VMEM)
+    pixels = rows * width
+    result = pl.pallas_call(
+        functools.partial(block_kernel, (n_frame, n_strip)),
+        out_shape=jax.ShapeDtypeStruct((rows, chans, width), bf16),
+        in_specs=[inside, inside] + [anywhere] * 7,
+        out_specs=inside,
+        scratch_shapes=[
+            pltpu.VMEM((rows + 2, 2, chans, width), bf16),
+            pltpu.VMEM((rows + 2, 3, 2, chans, width), bf16),
+            pltpu.VMEM((rows, chans, width), f32),
+            pltpu.VMEM((rows + 2, 3, chans, width), bf16),
+            pltpu.VMEM((rows, 3, chans, width), bf16),
+            pltpu.VMEM((chans, 128), f32),
+            pltpu.VMEM((chans, 128), f32),
+            pltpu.VMEM((2, 2, chans, 128), f32),
+            pltpu.VMEM((2, chans, 128), f32),
+            pltpu.VMEM((chans, 128), f32),
+            pltpu.VMEM((chans, 18 * chans), bf16),
+            pltpu.VMEM((3, 3, chans, chans), bf16),
+            pltpu.VMEM((chans, 9 * chans), bf16),
+            pltpu.VMEM((3, chans, chans), bf16),
+            pltpu.VMEM((chans, 3 * chans), bf16),
+            pltpu.VMEM((chans, 2 * chans), bf16),
+            pltpu.VMEM((chans, temb), bf16),
+            pltpu.VMEM((temb, temb), bf16),
+            pltpu.VMEM((temb, chans), bf16),
+            pltpu.VMEM((5, 8, 128), f32),
+            pltpu.VMEM((2, n_strip - 1, 8, 128), f32),
+            pltpu.VMEM((2, n_frame - 1, 8, 128), f32),
+            pltpu.VMEM((8, 128), f32),
+            dma((15,)), dma,
+            dma((rows,)), dma((rows,)),
+            dma((2,)), dma((2,)), dma((2,)), dma((2,)), dma((2,)), dma((2,)),
+            dma((2, rows)), dma((2, rows)),
+            dma((2, n_strip - 1)), dma((2, n_strip - 1)),
+            dma((2, n_frame - 1)), dma((2, n_frame - 1)),
+            dma, dma,
+        ],
+        compiler_params=pltpu.CompilerParams(
+            collective_id=0, has_side_effects=True, vmem_limit_bytes=58 * 2**20
+        ),
+        cost_estimate=pl.CostEstimate(
+            flops=2 * pixels * chans * chans * (18 + 9 + 3 + 2),
+            bytes_accessed=14 * 2**20,
+            transcendentals=pixels * chans * 4,
+        ),
+    )(feats, sinus, time_first, time_second, embed_proj, conv_first, conv_second, temporal_weight, skip_weight)
+    return result.reshape(rows, chans, frames, cols).transpose(1, 2, 0, 3)[None]
+
+
+def block(*args):
+    own, frames, rows, cols = args[0].shape
+    fits = (
+        lax.axis_size("step") == 2
+        and own % 16 == 0
+        and args[7].shape[2] == 2 * own
+        and (own * 4) % GROUPS == 0
+        and own % (own * 4 // GROUPS) == 0
+        and frames == 2
+        and rows == 8
+        and cols == 128
+    )
+    return in_kernel(*args) if fits else on_device(*args)
+
+
 def solution(mesh):
     return jax.shard_map(
-        on_device,
+        block,
         mesh=mesh,
         in_specs=(
             P("step", "frame", "strip", None),

time: 204 us -> 85.5 us (0.42)
  blocking collectives: 100 us -> 0 us
  Pallas kernels: 0 us -> 72.5 us
  matrix products: 37.4 us -> 0 us
  starting transfers between devices: 16.6 us -> 0 us
  between operations: 14.6 us -> 0.79 us
  other arithmetic: 12.8 us -> 0.25 us
  waiting for transfers between devices: 10.8 us -> 0 us
    psum x2 -> x0, blocking collectives: 100 us -> none  [the longest x1 57.3 us: on_device(): lax.psum((hidden_one, hidden_two), ('frame', 'strip'))]
    pallas_call x0 -> x1, Pallas kernels: none -> 72.5 us  [in_kernel(): pl.pallas_call(functools.partial(block_kernel, (n_frame, n_strip)), out_s...]
    dot_general x25 -> x0, matrix products: 37.4 us -> none  [the longest x18 30.2 us: conv_taps(): jnp.einsum('oi,ifhw->ofhw', weights[row_off, col_off], window, preferred_...]
    ppermute x6 -> x0, starting transfers between devices: 16.5 us -> none  [the longest x3 8.79 us: with_halo(): lax.ppermute(head, axis, [((i + 1) % count, i) for i in range(ends)])]
    ppermute x6 -> x0, waiting for transfers between devices: 10.8 us -> none  [the longest x3 6.98 us: with_halo(): lax.ppermute(tail, axis, [(i, (i + 1) % count) for i in range(ends)])]
    reshape x2 -> x3, local copies, waits for them, and re-layouts: 0.2 us -> 7.24 us  [the longest x2 5.53 us: in_kernel(): return result.reshape(rows, chans, frames, cols).transpose(1, 2, 0, 3)[None]]
    convert_element_type x5 -> x0, other arithmetic: 6.74 us -> none  [the longest x1 4.1 us: on_device(): normed.astype(jnp.bfloat16)]
    concatenate x3 -> x1, other arithmetic: 3.76 us -> 0.08 us  [in_kernel(): jnp.concatenate([jnp.cos(angle_rows), jnp.sin(angle_rows)], axis=1)]
  transfers between devices with their start and end apart: 7 -> 0, of which waited for: 3 -> 0; matrix products, arithmetic and copies ran while one was open for 7% -> 0% of each run, Pallas kernels for 0% -> 0%
where the time goes in v1:
time: 85.5 us; the launch traced here: 84.8 us
  Pallas kernels  72.5 us (85%)
  local copies, waits for them, and re-layouts  11.3 us (13%)
    pallas_call x1, Pallas kernels, in_kernel(): pl.pallas_call(functools.partial(block_kernel, (n_frame, n_strip)), out_s...  72.5 us
    reshape x2, local copies, waits for them, and re-layouts, in_kernel(): return result.reshape(rows, chans, frames, cols).transpose(1, 2, 0, 3)[None]  5.53 us
    unnamed x5, local copies, waits for them, and re-layouts  2.22 us

profile of v1, /device:TPU:1, one launch (start us, length us, event | category | flops | bytes accessed | tf_op | source)
XLA Modules:
  0.0 84.8 jit_solution(13518245982712032139)
XLA Ops:
  0.0 0.0 copy-start
  0.0 0.0 copy-start.1
  0.8 0.1 sine_convert_fusion
  0.8 0.1 pad_maximum_fusion
  0.9 0.6 broadcast_in_dim.4.sinus
  1.5 2.2 %copy.12.proj_h = bf16[1280,320]{1,0:T(8,128)(2,1)} copy(bf16[1280,320]{0,1:T(8,128)(2,1)} %param.15) | data formatting | bytes 1638400 | tf_op args[5]
  3.7 0.0 copy-done
  3.7 0.0 copy-done.1
  3.7 0.1 maximum_bitcast_fusion
  3.8 1.3 %copy.11 = bf16[8,2,160,2,128]{4,3,2,1,0:T(2,128)(2,1)S(1)} copy(bf16[8,2,160,2,128]{4,0,3,2,1:T(8,128)(2,1)S(1)} %maximum_bitcast_fusion) | data formatting | bytes 2621440 | tf_op jit(solution)/shard_map/transpose | solution.py:611
  5.1 1.7 %reshape.30.feats = bf16[8,2,160,256]{3,2,1,0:T(8,128)(2,1)} reshape(bf16[8,2,160,2,128]{4,3,2,1,0:T(2,128)(2,1)S(1)} %copy.11) | data formatting | bytes 2621440 | tf_op jit(solution)/shard_map/reshape | solution.py:611
  6.8 72.5 %shard_map.100 = bf16[8,320,256]{2,1,0:T(8,128)(2,1)} custom-call(bf16[8,2,160,256]{3,2,1,0:T(8,128)(2,1)} %reshape.30.feats, bf16[16,320]{1,0:T(8,128)(2,1)} %broadcast_in_dim.4.sinus, bf16[320,1280]{1,0:T(8,128)(2,1)} %first_h.1, bf16[1280,1280]{1,0:T(8,128)(2,1)} %second_h.1, bf16[1280,320]{1,0:T(8,128)(2,1)} %copy.12.proj_h, ...), custom_call_target="tpu_custom_call" | custom-call | flops 13421772800 | bytes 14680064 | tf_op jit(solution)/shard_map/pallas_call | solution.py:624
  79.3 3.0 %reshape.31 = bf16[8,320,2,128]{3,2,1,0:T(2,128)(2,1)S(1)} reshape(bf16[8,320,256]{2,1,0:T(8,128)(2,1)} %shard_map.100) | data formatting | bytes 2621440 | tf_op jit(solution)/shard_map/reshape | solution.py:670
  82.3 2.6 %copy.15 = bf16[8,320,2,128]{3,0,2,1:T(8,128)(2,1)} copy(bf16[8,320,2,128]{3,2,1,0:T(2,128)(2,1)S(1)} %reshape.31) | data formatting | bytes 2621440 | tf_op jit(solution)/shard_map/reshape | solution.py:670
Async XLA Ops:
  0.0 3.7 %copy-start = (bf16[160,2,8,128]{3,2,1,0:T(8,128)(2,1)S(1)}, bf16[160,2,8,128]{3,2,1,0:T(8,128)(2,1)}, u32[]{:S(2)}) copy-start(bf16[160,2,8,128]{3,2,1,0:T(8,128)(2,1)} %param.11) | copy-start | bytes 1966084
  0.0 3.7 %copy-start.1 = (bf16[160,2,8,128]{3,2,1,0:T(8,128)(2,1)S(1)}, bf16[160,2,8,128]{3,2,1,0:T(8,128)(2,1)}, u32[]{:S(2)}) copy-start(bf16[160,2,8,128]{3,2,1,0:T(8,128)(2,1)} %param.10) | copy-start | bytes 1966084

commit v2 on v1

--- a/solution.py
+++ b/solution.py
@@ -244,16 +244,21 @@
     return total
 
 
-def put_taps(value, store):
-    lane = lax.broadcasted_iota(jnp.int32, value.shape, 1)
-    store(0, jnp.where(lane == 0, 0.0, pltpu.roll(value, 1, 1)).astype(jnp.bfloat16))
-    store(1, value.astype(jnp.bfloat16))
-    store(2, jnp.where(lane == 127, 0.0, pltpu.roll(value, 127, 1)).astype(jnp.bfloat16))
+def join_taps(found, chans, f):
+    lanes = slice(f * 128, f * 128 + 128)
+    lane = lax.broadcasted_iota(jnp.int32, (chans, 128), 1)
+    before = pltpu.roll(found[:chans, lanes], 1, 1)
+    after = pltpu.roll(found[2 * chans :, lanes], 127, 1)
+    return (
+        found[chans : 2 * chans, lanes]
+        + jnp.where(lane == 0, 0.0, before)
+        + jnp.where(lane == 127, 0.0, after)
+    )
 
 
 def block_kernel(
     sizes,
-    feats, sinus, first_h, second_h, proj_h, conv1_h, conv2_h, temp_h, skip_h,
+    enc, skip, sinus, first_h, second_h, proj_h, conv1_h, conv2_h, temp_h, skip_h,
     out,
     raw, act, hid, act2, tbuf, acc1, acc2, cols_in, cols_mid, emb,
     w1, w2raw, w2, wtraw, wt, ws, tf, ts, ep,
@@ -262,7 +267,7 @@
     t_send, t_recv, ss_send, ss_recv, sf_send, sf_recv, sx_send, sx_recv,
 ):
     n_frame, n_strip = sizes
-    rows, own = feats.shape[0], feats.shape[2]
+    rows, own = enc.shape[1], enc.shape[2]
     chans = 2 * own
     last = rows - 1
     step, frame, strip = (lax.axis_index(a) for a in ("step", "frame", "strip"))
@@ -271,7 +276,7 @@
     theirs = pl.ds(pl.multiple_of(partner * own, 16), own)
 
     loads = [
-        pltpu.make_async_copy(conv1_h.at[t // 3, t % 3], w1.at[:, pl.ds(t * 2 * chans, 2 * chans)], wsem.at[t])
+        pltpu.make_async_copy(conv1_h.at[t // 3, t % 3], w1.at[pl.ds(t % 3 * chans, chans), pl.ds(t // 3 * 2 * chans, 2 * chans)], wsem.at[t])
         for t in range(9)
     ]
     small = [
@@ -280,8 +285,15 @@
             ((first_h, tf), (second_h, ts), (proj_h, ep), (conv2_h, w2raw), (temp_h, wtraw), (skip_h, ws))
         )
     ]
-    keep = pltpu.make_async_copy(feats, raw.at[pl.ds(1, rows), :, mine, :], own_sem)
-    keep.start()
+    keeps = [
+        pltpu.make_async_copy(
+            source.at[f], raw.at[pl.ds(1, rows), h, mine, pl.ds(f * 128, 128)], own_sem.at[h, f]
+        )
+        for h, source in enumerate((enc, skip))
+        for f in range(2)
+    ]
+    for keep in keeps:
+        keep.start()
 
     barrier = pltpu.get_barrier_semaphore()
     for axis, n in (("step", 2), ("frame", n_frame), ("strip", n_strip)):
@@ -290,15 +302,17 @@
                 barrier, inc=1, device_id={axis: lax.rem(lax.axis_index(axis) + d, n)}, device_id_type=MESH
             )
     pl.semaphore_wait(barrier, 1 + n_frame - 1 + n_strip - 1)
+    for keep in keeps:
+        keep.wait()
 
     def row_copy(r):
-        return push(feats.at[r], raw.at[r + 1, :, mine, :], x_send.at[r], x_recv.at[r], "step", partner)
+        return push(raw.at[r + 1, :, mine, :], raw.at[r + 1, :, mine, :], x_send.at[r], x_recv.at[r], "step", partner)
 
     def own_up():
-        return push(feats.at[0], raw.at[rows + 1, :, mine, :], h_send.at[1], h_recv.at[1], "strip", strip - 1)
+        return push(raw.at[1, :, mine, :], raw.at[rows + 1, :, mine, :], h_send.at[1], h_recv.at[1], "strip", strip - 1)
 
     def own_down():
-        return push(feats.at[last], raw.at[0, :, mine, :], h_send.at[0], h_recv.at[0], "strip", strip + 1)
+        return push(raw.at[rows, :, mine, :], raw.at[0, :, mine, :], h_send.at[0], h_recv.at[0], "strip", strip + 1)
 
     def far_up():
         return push(
@@ -329,7 +343,7 @@
     @pl.loop(0, rows)
     def _(r):
         for h in range(2):
-            wide = feats[r, h].astype(jnp.float32)
+            wide = raw[r + 1, h, mine, :].astype(jnp.float32)
             a, b = wide[:, :128], wide[:, 128:]
             at = pl.ds(h * own, own)
             acc1[at, :] = acc1[at, :] + (a + b)
@@ -358,13 +372,7 @@
             for f in range(2):
                 lanes = pl.ds(f * 128, 128)
                 value = silu((raw[r, h, at, lanes].astype(jnp.float32) - mean) * rstd)
-
-                def store(t, v):
-                    act[r, t, h, at, lanes] = v
-
-                put_taps(value, store)
-
-    keep.wait()
+                act[r, h, at, lanes] = value.astype(jnp.bfloat16)
 
     @pl.loop(1, rows + 1)
     def _(r):
@@ -395,12 +403,13 @@
         load.wait()
     one = silu(jnp.dot(sinus[...], tf[...], preferred_element_type=jnp.float32)).astype(jnp.bfloat16)
     two = silu(jnp.dot(one, ts[...], preferred_element_type=jnp.float32)).astype(jnp.bfloat16)
-    embed = jnp.dot(two, ep[...], preferred_element_type=jnp.float32)
-    emb[...] = jnp.broadcast_to(
-        lane_dot(one_hot((chans, chans), 0, 1, 0), embed[:8])[:, :1], (chans, 128)
-    )
+    embed = lax.dot_general(
+        ep[...], two, (((1,), (1,)), ((), ())), preferred_element_type=jnp.float32
+    )
+    emb[...] = jnp.broadcast_to(embed[:, :1], (chans, 128))
     for t in range(9):
-        w2[:, t * chans : (t + 1) * chans] = w2raw[t // 3, t % 3]
+        dy, dx = t // 3, t % 3
+        w2[dx * chans : (dx + 1) * chans, dy * chans : (dy + 1) * chans] = w2raw[dy, dx]
     for t in range(3):
         wt[:, t * chans : (t + 1) * chans] = wtraw[t]
     for load in loads:
@@ -438,9 +447,9 @@
             far_up().wait_recv()
             make_act(rows + 1, theirs)
 
-        window = act[pl.ds(c, 3)].reshape(18 * chans, 256)
+        window = act[pl.ds(c, 3)].reshape(6 * chans, 256)
         found = jnp.dot(w1[...], window, preferred_element_type=jnp.float32)
-        a, b = found[:, :128] + emb[...], found[:, 128:] + emb[...]
+        a, b = join_taps(found, chans, 0) + emb[...], join_taps(found, chans, 1) + emb[...]
         hid[c, :, :128] = a
         hid[c, :, 128:] = b
         acc1[...] = acc1[...] + (a + b)
@@ -458,17 +467,13 @@
         for f in range(2):
             lanes = pl.ds(f * 128, 128)
             value = silu((hid[r, :, lanes] - cols_mid[0]) * cols_mid[1])
-
-            def store(t, v):
-                act2[r + 1, t, :, lanes] = v
-
-            put_taps(value, store)
+            act2[r + 1, :, lanes] = value.astype(jnp.bfloat16)
 
     def mid_up():
-        return push(act2.at[1, 1], act2.at[rows + 1, 1], m_send.at[1], m_recv.at[1], "strip", strip - 1)
+        return push(act2.at[1], act2.at[rows + 1], m_send.at[1], m_recv.at[1], "strip", strip - 1)
 
     def mid_down():
-        return push(act2.at[rows, 1], act2.at[0, 1], m_send.at[0], m_recv.at[0], "strip", strip + 1)
+        return push(act2.at[rows], act2.at[0], m_send.at[0], m_recv.at[0], "strip", strip + 1)
 
     mid_row(0)
     pl.when(has_up)(lambda: mid_up().start())
@@ -479,17 +484,6 @@
     def _(r):
         mid_row(r)
 
-    def edge_row(r):
-        for f in range(2):
-            lanes = pl.ds(f * 128, 128)
-            value = act2[r, 1, :, lanes].astype(jnp.float32)
-
-            def store(t, v):
-                if t != 1:
-                    act2[r, t, :, lanes] = v
-
-            put_taps(value, store)
-
     has_prev, has_next = frame > 0, frame < n_frame - 1
 
     def to_prev(c):
@@ -515,12 +509,10 @@
         @pl.when((i == rows - 2) & has_up)
         def _():
             mid_down().wait_recv()
-            edge_row(0)
 
         @pl.when((i == rows - 2) & has_down)
         def _():
             mid_up().wait_recv()
-            edge_row(rows + 1)
 
         @pl.when((i == rows - 2) & (strip == 0))
         def _():
@@ -530,13 +522,15 @@
         def _():
             act2[rows + 1] = jnp.zeros(act2.shape[1:], jnp.bfloat16)
 
-        window = act2[pl.ds(c, 3)].reshape(9 * chans, 256)
+        window = act2[pl.ds(c, 3)].reshape(3 * chans, 256)
         found = jnp.dot(w2[...], window, preferred_element_type=jnp.float32)
-        hid[c] = found
-        inner = silu(found).astype(jnp.bfloat16)
-        tbuf[c, 1] = inner
-        tbuf[c, 0, :, 128:] = inner[:, :128]
-        tbuf[c, 2, :, :128] = inner[:, 128:]
+        for f in range(2):
+            lanes = pl.ds(f * 128, 128)
+            second = join_taps(found, chans, f)
+            hid[c, :, lanes] = second
+            inner = silu(second).astype(jnp.bfloat16)
+            tbuf[c, 1, :, lanes] = inner
+            tbuf[c, 2 * f, :, pl.ds(128 - f * 128, 128)] = inner
 
         @pl.when(has_prev)
         def _():
@@ -572,7 +566,9 @@
         mixed = jnp.dot(
             wt[...], tbuf[c].reshape(3 * chans, 256), preferred_element_type=jnp.float32
         )
-        out[c] = (base + mixed).astype(jnp.bfloat16)
+        result = (base + mixed).astype(jnp.bfloat16)
+        out[0, c] = result[:, :128]
+        out[1, c] = result[:, 128:]
 
     @pl.loop(0, rows)
     def _(r):
@@ -608,7 +604,7 @@
     width = frames * cols
     temb = time_first.shape[1]
     n_frame, n_strip = lax.axis_size("frame"), lax.axis_size("strip")
-    feats = jnp.stack([enc_feats, skip_feats]).transpose(3, 0, 1, 2, 4).reshape(rows, 2, own, width)
+    enc, skip = (part.transpose(1, 2, 0, 3) for part in (enc_feats, skip_feats))
     half_chans = chans // 2
     freq_table = jnp.exp(
         -math.log(10000.0) * jnp.arange(half_chans, dtype=jnp.float32) / half_chans
@@ -623,34 +619,34 @@
     pixels = rows * width
     result = pl.pallas_call(
         functools.partial(block_kernel, (n_frame, n_strip)),
-        out_shape=jax.ShapeDtypeStruct((rows, chans, width), bf16),
-        in_specs=[inside, inside] + [anywhere] * 7,
+        out_shape=jax.ShapeDtypeStruct((frames, rows, chans, cols), bf16),
+        in_specs=[anywhere, anywhere, inside] + [anywhere] * 7,
         out_specs=inside,
         scratch_shapes=[
             pltpu.VMEM((rows + 2, 2, chans, width), bf16),
-            pltpu.VMEM((rows + 2, 3, 2, chans, width), bf16),
+            pltpu.VMEM((rows + 2, 2, chans, width), bf16),
             pltpu.VMEM((rows, chans, width), f32),
-            pltpu.VMEM((rows + 2, 3, chans, width), bf16),
+            pltpu.VMEM((rows + 2, chans, width), bf16),
             pltpu.VMEM((rows, 3, chans, width), bf16),
             pltpu.VMEM((chans, 128), f32),
             pltpu.VMEM((chans, 128), f32),
             pltpu.VMEM((2, 2, chans, 128), f32),
             pltpu.VMEM((2, chans, 128), f32),
             pltpu.VMEM((chans, 128), f32),
-            pltpu.VMEM((chans, 18 * chans), bf16),
+            pltpu.VMEM((3 * chans, 6 * chans), bf16),
             pltpu.VMEM((3, 3, chans, chans), bf16),
-            pltpu.VMEM((chans, 9 * chans), bf16),
+            pltpu.VMEM((3 * chans, 3 * chans), bf16),
             pltpu.VMEM((3, chans, chans), bf16),
             pltpu.VMEM((chans, 3 * chans), bf16),
             pltpu.VMEM((chans, 2 * chans), bf16),
             pltpu.VMEM((chans, temb), bf16),
             pltpu.VMEM((temb, temb), bf16),
-            pltpu.VMEM((temb, chans), bf16),
+            pltpu.VMEM((chans, temb), bf16),
             pltpu.VMEM((5, 8, 128), f32),
             pltpu.VMEM((2, n_strip - 1, 8, 128), f32),
             pltpu.VMEM((2, n_frame - 1, 8, 128), f32),
             pltpu.VMEM((8, 128), f32),
-            dma((15,)), dma,
+            dma((15,)), dma((2, 2)),
             dma((rows,)), dma((rows,)),
             dma((2,)), dma((2,)), dma((2,)), dma((2,)), dma((2,)), dma((2,)),
             dma((2, rows)), dma((2, rows)),
@@ -666,8 +662,8 @@
             bytes_accessed=14 * 2**20,
             transcendentals=pixels * chans * 4,
         ),
-    )(feats, sinus, time_first, time_second, embed_proj, conv_first, conv_second, temporal_weight, skip_weight)
-    return result.reshape(rows, chans, frames, cols).transpose(1, 2, 0, 3)[None]
+    )(enc, skip, sinus, time_first, time_second, embed_proj.T, conv_first, conv_second, temporal_weight, skip_weight)
+    return result.transpose(2, 0, 1, 3)[None]
 
 
 def block(*args):

time: 85.5 us -> 79.3 us (0.927)
  local copies, waits for them, and re-layouts: 11.3 us -> 6.54 us
  Pallas kernels: 72.5 us -> 71.3 us
    reshape x3 -> x0, local copies, waits for them, and re-layouts: 7.24 us -> none  [the longest x2 5.53 us: in_kernel(): return result.reshape(rows, chans, frames, cols).transpose(1, 2, 0, 3)[None]]
    broadcast_in_dim x0 -> x1, local copies, waits for them, and re-layouts: none -> 3.22 us  [in_kernel(): return result.transpose(2, 0, 1, 3)[None]]
    unnamed x5 -> x0, local copies, waits for them, and re-layouts: 2.22 us -> none
    transpose x1, local copies, waits for them, and re-layouts: 1.26 us -> 2.71 us  [in_kernel(): enc, skip = (part.transpose(1, 2, 0, 3) for part in (enc_feats, skip_feats))]
    pallas_call x1, Pallas kernels: 72.5 us -> 71.3 us  [in_kernel(): pl.pallas_call(functools.partial(block_kernel, (n_frame, n_strip)), out_s...]
where the time goes in v2:
time: 79.3 us; the launch traced here: 78.7 us
  Pallas kernels  71.3 us (90%)
  local copies, waits for them, and re-layouts  6.54 us (8%)
    pallas_call x1, Pallas kernels, in_kernel(): pl.pallas_call(functools.partial(block_kernel, (n_frame, n_strip)), out_s...  71.3 us
    broadcast_in_dim x1, local copies, waits for them, and re-layouts, in_kernel(): return result.transpose(2, 0, 1, 3)[None]  3.22 us
    transpose x1, local copies, waits for them, and re-layouts, in_kernel(): enc, skip = (part.transpose(1, 2, 0, 3) for part in (enc_feats, skip_feats))  2.71 us

profile of v2, /device:TPU:1, one launch (start us, length us, event | category | flops | bytes accessed | tf_op | source)
XLA Modules:
  0.0 78.7 jit_solution(3738218022932866097)
XLA Ops:
  0.7 0.1 sine_convert_fusion
  0.7 0.1 pad_maximum_fusion
  0.8 0.6 broadcast_in_dim.4.sinus
  1.4 2.7 %copy_bitcast_fusion = (bf16[2,8,160,128]{3,2,1,0:T(8,128)(2,1)}, bf16[2,8,160,128]{3,2,1,0:T(8,128)(2,1)}) fusion(bf16[160,2,8,128]{3,2,1,0:T(8,128)(2,1)} %param.11, bf16[160,2,8,128]{3,2,1,0:T(8,128)(2,1)} %param.10), kind=kLoop, calls=%fused_computation | loop fusion | bytes 2621440 | tf_op jit(solution)/shard_map/transpose | solution.py:607
  4.1 71.3 %shard_map.100 = bf16[2,8,320,128]{3,2,1,0:T(8,128)(2,1)} custom-call(bf16[2,8,160,128]{3,2,1,0:T(8,128)(2,1)} %get-tuple-element.8.enc, bf16[2,8,160,128]{3,2,1,0:T(8,128)(2,1)} %get-tuple-element.7.skip, bf16[16,320]{1,0:T(8,128)(2,1)} %broadcast_in_dim.4.sinus, bf16[320,1280]{1,0:T(8,128)(2,1)} %first_h.1, bf16[1280,1280]{1,0:T(8,128)(2,1)} %second_h.1, ...), custom_call_target="tpu_custom_call" | custom-call | flops 13421772800 | bytes 14680064 | tf_op jit(solution)/shard_map/pallas_call | solution.py:620
  75.4 3.2 %copy.13 = bf16[1,320,2,8,128]{4,3,2,1,0:T(8,128)(2,1)} copy(bf16[1,320,2,8,128]{4,1,3,2,0:T(8,128)(2,1)} %bitcast.9) | data formatting | bytes 2621440 | tf_op jit(solution)/shard_map/broadcast_in_dim | solution.py:666

commit v3 on v2

--- a/solution.py
+++ b/solution.py
@@ -227,20 +227,34 @@
     )
 
 
-def sum_over(axis, n, src, slots, send, recv):
-    me = lax.axis_index(axis)
+def peers_of(n_frame, n_strip):
+    frame, strip = lax.axis_index("frame"), lax.axis_index("strip")
+    return [
+        {"frame": lax.rem(frame + df, n_frame), "strip": lax.rem(strip + ds, n_strip)}
+        for df in range(n_frame)
+        for ds in range(n_strip)
+        if df or ds
+    ]
+
+
+def send_all(src, slots, send, recv, peers):
     copies = [
-        push(src, slots.at[d - 1], send.at[d - 1], recv.at[d - 1], axis, lax.rem(me + d, n))
-        for d in range(1, n)
+        pltpu.make_async_remote_copy(
+            src_ref=src, dst_ref=slots.at[d], send_sem=send.at[d], recv_sem=recv.at[d],
+            device_id=peer, device_id_type=MESH,
+        )
+        for d, peer in enumerate(peers)
     ]
     for copy in copies:
         copy.start()
+    return copies
+
+
+def add_all(src, slots, copies):
     total = src[...]
     for d, copy in enumerate(copies):
         copy.wait_recv()
         total = total + slots[d]
-    for copy in copies:
-        copy.wait_send()
     return total
 
 
@@ -260,11 +274,11 @@
     sizes,
     enc, skip, sinus, first_h, second_h, proj_h, conv1_h, conv2_h, temp_h, skip_h,
     out,
-    raw, act, hid, act2, tbuf, acc1, acc2, cols_in, cols_mid, emb,
+    raw, act, hid, skipped, act2, tbuf, acc1, acc2, cols_in, cols_mid, emb,
     w1, w2raw, w2, wtraw, wt, ws, tf, ts, ep,
-    stats, slots_strip, slots_frame, slot_step,
+    stats, slots, slot_step,
     wsem, own_sem, x_send, x_recv, h_send, h_recv, g_send, g_recv, m_send, m_recv,
-    t_send, t_recv, ss_send, ss_recv, sf_send, sf_recv, sx_send, sx_recv,
+    t_send, t_recv, s_send, s_recv, sx_send, sx_recv,
 ):
     n_frame, n_strip = sizes
     rows, own = enc.shape[1], enc.shape[2]
@@ -275,10 +289,7 @@
     mine = pl.ds(pl.multiple_of(step * own, 16), own)
     theirs = pl.ds(pl.multiple_of(partner * own, 16), own)
 
-    loads = [
-        pltpu.make_async_copy(conv1_h.at[t // 3, t % 3], w1.at[pl.ds(t % 3 * chans, chans), pl.ds(t // 3 * 2 * chans, 2 * chans)], wsem.at[t])
-        for t in range(9)
-    ]
+    loads = [pltpu.make_async_copy(conv1_h, w1, wsem.at[0])]
     small = [
         pltpu.make_async_copy(src, dst, wsem.at[9 + i])
         for i, (src, dst) in enumerate(
@@ -296,12 +307,10 @@
         keep.start()
 
     barrier = pltpu.get_barrier_semaphore()
-    for axis, n in (("step", 2), ("frame", n_frame), ("strip", n_strip)):
-        for d in range(1, n):
-            pl.semaphore_signal(
-                barrier, inc=1, device_id={axis: lax.rem(lax.axis_index(axis) + d, n)}, device_id_type=MESH
-            )
-    pl.semaphore_wait(barrier, 1 + n_frame - 1 + n_strip - 1)
+    peers = peers_of(n_frame, n_strip)
+    for peer in peers + [{"step": partner}]:
+        pl.semaphore_signal(barrier, inc=1, device_id=peer, device_id_type=MESH)
+    pl.semaphore_wait(barrier, len(peers) + 1)
     for keep in keeps:
         keep.wait()
 
@@ -351,9 +360,9 @@
 
     per_in = 2 * chans // GROUPS
     stats[0] = pack_sums(acc1[...], acc2[...], per_in)
-    stats[1] = sum_over("strip", n_strip, stats.at[0], slots_strip.at[0], ss_send.at[0], ss_recv.at[0])
-    stats[2] = sum_over("frame", n_frame, stats.at[1], slots_frame.at[0], sf_send.at[0], sf_recv.at[0])
-    swap = push(stats.at[2], slot_step, sx_send, sx_recv, "step", partner)
+    sent = send_all(stats.at[0], slots.at[0], s_send.at[0], s_recv.at[0], peers)
+    stats[1] = add_all(stats.at[0], slots.at[0], sent)
+    swap = push(stats.at[1], slot_step, sx_send, sx_recv, "step", partner)
     swap.start()
     entries = 2 * rows * 128 * n_frame * n_strip
     in_entries = float(entries * per_in)
@@ -364,7 +373,7 @@
             cols_in[0, h, at, :] = mean[h * own : (h + 1) * own]
             cols_in[1, h, at, :] = rstd[h * own : (h + 1) * own]
 
-    set_cols(stats[2], mine)
+    set_cols(stats[1], mine)
 
     def make_act(r, at):
         for h in range(2):
@@ -388,20 +397,13 @@
         own_up().wait_recv()
         make_act(rows + 1, mine)
 
-    @pl.when(strip == 0)
-    def _():
-        act[0] = jnp.zeros(act.shape[1:], jnp.bfloat16)
-
-    @pl.when(strip == n_strip - 1)
-    def _():
-        act[rows + 1] = jnp.zeros(act.shape[1:], jnp.bfloat16)
-
     swap.wait()
     set_cols(slot_step[...], theirs)
 
     for load in small:
         load.wait()
-    one = silu(jnp.dot(sinus[...], tf[...], preferred_element_type=jnp.float32)).astype(jnp.bfloat16)
+    one = silu(jnp.dot(
+        jnp.broadcast_to(sinus[...].astype(jnp.float32), (16, chans)).astype(jnp.bfloat16), tf[...], preferred_element_type=jnp.float32)).astype(jnp.bfloat16)
     two = silu(jnp.dot(one, ts[...], preferred_element_type=jnp.float32)).astype(jnp.bfloat16)
     embed = lax.dot_general(
         ep[...], two, (((1,), (1,)), ((), ())), preferred_element_type=jnp.float32
@@ -415,50 +417,78 @@
     for load in loads:
         load.wait()
 
-    def arrive(r):
+    start_value = jnp.concatenate([emb[...], emb[...]], axis=1)
+
+    @pl.loop(0, rows + 4)
+    def _(r):
+        hid[r] = start_value
+
+    def add_taps(r, offsets):
+        image_row = act[r].reshape(2 * chans, 256)
+        for dy in offsets:
+            found = jnp.dot(
+                w1[dy].reshape(3 * chans, 2 * chans), image_row, preferred_element_type=jnp.float32
+            )
+            for f in range(2):
+                lanes = pl.ds(f * 128, 128)
+                hid[r - dy + 2, :, lanes] = hid[r - dy + 2, :, lanes] + join_taps(found, chans, f)
+
+    def add_skip(r):
+        skipped[r] = jnp.dot(
+            ws[...], raw[r + 1].reshape(2 * chans, 256), preferred_element_type=jnp.float32
+        )
+
+    def arrival(i):
+        later = (i + rows - 2) // rows
+        return (i - 1) * later + last * i * (1 - later)
+
+    @pl.loop(0, rows)
+    def _(i):
+        r = arrival(i)
+
+        @pl.when(i > 0)
+        def _():
+            add_skip(arrival(i - 1))
+
         row_copy(r).wait_recv()
+
+        @pl.when((i == 0) & has_up)
+        def _():
+            far_up().start()
+
+        @pl.when((i == 1) & has_down)
+        def _():
+            far_down().start()
+
         make_act(r + 1, theirs)
-
-    arrive(0)
-    pl.when(has_up)(lambda: far_up().start())
-    arrive(last)
-    pl.when(has_down)(lambda: far_down().start())
-    arrive(1)
+        add_taps(r + 1, (0, 1, 2))
+
+        @pl.when((i == rows - 3) & has_up)
+        def _():
+            far_down().wait_recv()
+            make_act(0, theirs)
+            add_taps(0, (0,))
+
+        @pl.when((i == rows - 3) & has_down)
+        def _():
+            far_up().wait_recv()
+            make_act(rows + 1, theirs)
+            add_taps(rows + 1, (2,))
+
     acc1[...] = jnp.zeros_like(acc1)
     acc2[...] = jnp.zeros_like(acc2)
 
     @pl.loop(0, rows)
-    def _(i):
-        high = i // 4
-        three = (i // 3) % 2 * (1 - high)
-        c = (i + 1) * (1 - high) * (1 - three) + i * high
-
-        @pl.when((i < 3) | ((i > 3) & (i < rows - 2)))
-        def _():
-            arrive(c + 1)
-
-        @pl.when((i == 3) & has_up)
-        def _():
-            far_down().wait_recv()
-            make_act(0, theirs)
-
-        @pl.when((i == 3) & has_down)
-        def _():
-            far_up().wait_recv()
-            make_act(rows + 1, theirs)
-
-        window = act[pl.ds(c, 3)].reshape(6 * chans, 256)
-        found = jnp.dot(w1[...], window, preferred_element_type=jnp.float32)
-        a, b = join_taps(found, chans, 0) + emb[...], join_taps(found, chans, 1) + emb[...]
-        hid[c, :, :128] = a
-        hid[c, :, 128:] = b
+    def _(c):
+        a, b = hid[c + 2, :, :128], hid[c + 2, :, 128:]
         acc1[...] = acc1[...] + (a + b)
         acc2[...] = acc2[...] + (a * a + b * b)
 
     per_mid = chans // GROUPS
-    stats[3] = pack_sums(acc1[...], acc2[...], per_mid)
-    stats[4] = sum_over("strip", n_strip, stats.at[3], slots_strip.at[1], ss_send.at[1], ss_recv.at[1])
-    total = sum_over("frame", n_frame, stats.at[4], slots_frame.at[1], sf_send.at[1], sf_recv.at[1])
+    stats[2] = pack_sums(acc1[...], acc2[...], per_mid)
+    sent_mid = send_all(stats.at[2], slots.at[1], s_send.at[1], s_recv.at[1], peers)
+    add_skip(last - 1)
+    total = add_all(stats.at[2], slots.at[1], sent_mid)
     mean, rstd = columns_of(total, chans, per_mid, float(entries * per_mid))
     cols_mid[0] = mean
     cols_mid[1] = rstd
@@ -466,7 +496,7 @@
     def mid_row(r):
         for f in range(2):
             lanes = pl.ds(f * 128, 128)
-            value = silu((hid[r, :, lanes] - cols_mid[0]) * cols_mid[1])
+            value = silu((hid[r + 2, :, lanes] - cols_mid[0]) * cols_mid[1])
             act2[r + 1, :, lanes] = value.astype(jnp.bfloat16)
 
     def mid_up():
@@ -551,9 +581,7 @@
     @pl.loop(0, rows)
     def _(i):
         c = inner_first(i)
-        base = hid[c] + jnp.dot(
-            ws[...], raw[c + 1].reshape(2 * chans, 256), preferred_element_type=jnp.float32
-        )
+        base = hid[c] + skipped[c]
 
         @pl.when(has_prev)
         def _():
@@ -581,6 +609,9 @@
         @pl.when(has_next)
         def _():
             to_next(r).wait_send()
+
+    for copy in sent + sent_mid:
+        copy.wait_send()
 
     @pl.when(has_up)
     def _():
@@ -605,13 +636,13 @@
     temb = time_first.shape[1]
     n_frame, n_strip = lax.axis_size("frame"), lax.axis_size("strip")
     enc, skip = (part.transpose(1, 2, 0, 3) for part in (enc_feats, skip_feats))
+    n_peer = n_frame * n_strip - 1
     half_chans = chans // 2
     freq_table = jnp.exp(
         -math.log(10000.0) * jnp.arange(half_chans, dtype=jnp.float32) / half_chans
     )
     angle_rows = timesteps.astype(jnp.float32)[:, None] * freq_table[None, :]
     sinus = jnp.concatenate([jnp.cos(angle_rows), jnp.sin(angle_rows)], axis=1).astype(jnp.bfloat16)
-    sinus = jnp.broadcast_to(sinus, (16, chans))
     bf16, f32 = jnp.bfloat16, jnp.float32
     dma = pltpu.SemaphoreType.DMA
     anywhere = pl.BlockSpec(memory_space=pl.ANY)
@@ -625,6 +656,7 @@
         scratch_shapes=[
             pltpu.VMEM((rows + 2, 2, chans, width), bf16),
             pltpu.VMEM((rows + 2, 2, chans, width), bf16),
+            pltpu.VMEM((rows + 4, chans, width), f32),
             pltpu.VMEM((rows, chans, width), f32),
             pltpu.VMEM((rows + 2, chans, width), bf16),
             pltpu.VMEM((rows, 3, chans, width), bf16),
@@ -633,7 +665,7 @@
             pltpu.VMEM((2, 2, chans, 128), f32),
             pltpu.VMEM((2, chans, 128), f32),
             pltpu.VMEM((chans, 128), f32),
-            pltpu.VMEM((3 * chans, 6 * chans), bf16),
+            pltpu.VMEM((3, 3, chans, 2 * chans), bf16),
             pltpu.VMEM((3, 3, chans, chans), bf16),
             pltpu.VMEM((3 * chans, 3 * chans), bf16),
             pltpu.VMEM((3, chans, chans), bf16),
@@ -642,16 +674,14 @@
             pltpu.VMEM((chans, temb), bf16),
             pltpu.VMEM((temb, temb), bf16),
             pltpu.VMEM((chans, temb), bf16),
-            pltpu.VMEM((5, 8, 128), f32),
-            pltpu.VMEM((2, n_strip - 1, 8, 128), f32),
-            pltpu.VMEM((2, n_frame - 1, 8, 128), f32),
+            pltpu.VMEM((3, 8, 128), f32),
+            pltpu.VMEM((2, n_peer, 8, 128), f32),
             pltpu.VMEM((8, 128), f32),
             dma((15,)), dma((2, 2)),
             dma((rows,)), dma((rows,)),
             dma((2,)), dma((2,)), dma((2,)), dma((2,)), dma((2,)), dma((2,)),
             dma((2, rows)), dma((2, rows)),
-            dma((2, n_strip - 1)), dma((2, n_strip - 1)),
-            dma((2, n_frame - 1)), dma((2, n_frame - 1)),
+            dma((2, n_peer)), dma((2, n_peer)),
             dma, dma,
         ],
         compiler_params=pltpu.CompilerParams(

time: 79.3 us -> 81 us (1.021)
  Pallas kernels: 71.3 us -> 73.5 us
    pallas_call x1, Pallas kernels: 71.3 us -> 73.5 us  [in_kernel(): pl.pallas_call(functools.partial(block_kernel, (n_frame, n_strip)), out_s...]
where the time goes in v3:
time: 81 us; the launch traced here: 80.8 us
  Pallas kernels  73.5 us (91%)
  local copies, waits for them, and re-layouts  5.94 us (7%)
    pallas_call x1, Pallas kernels, in_kernel(): pl.pallas_call(functools.partial(block_kernel, (n_frame, n_strip)), out_s...  73.5 us
    broadcast_in_dim x1, local copies, waits for them, and re-layouts, in_kernel(): return result.transpose(2, 0, 1, 3)[None]  3.22 us
    transpose x1, local copies, waits for them, and re-layouts, in_kernel(): enc, skip = (part.transpose(1, 2, 0, 3) for part in (enc_feats, skip_feats))  2.71 us

profile of v3, /device:TPU:1, one launch (start us, length us, event | category | flops | bytes accessed | tf_op | source)
XLA Modules:
  0.0 80.8 jit_solution(112063748469060373)
XLA Ops:
  0.7 0.1 sine_convert_fusion
  0.7 0.6 pad_maximum_fusion.sinus
  1.4 2.7 %copy_bitcast_fusion = (bf16[2,8,160,128]{3,2,1,0:T(8,128)(2,1)}, bf16[2,8,160,128]{3,2,1,0:T(8,128)(2,1)}) fusion(bf16[160,2,8,128]{3,2,1,0:T(8,128)(2,1)} %param.11, bf16[160,2,8,128]{3,2,1,0:T(8,128)(2,1)} %param.10), kind=kLoop, calls=%fused_computation | loop fusion | bytes 2621440 | tf_op jit(solution)/shard_map/transpose | solution.py:638
  4.1 73.5 %shard_map.100 = bf16[2,8,320,128]{3,2,1,0:T(8,128)(2,1)} custom-call(bf16[2,8,160,128]{3,2,1,0:T(8,128)(2,1)} %get-tuple-element.8.enc, bf16[2,8,160,128]{3,2,1,0:T(8,128)(2,1)} %get-tuple-element.7.skip, bf16[1,320]{1,0:T(2,128)(2,1)} %pad_maximum_fusion.sinus, bf16[320,1280]{1,0:T(8,128)(2,1)} %first_h.1, bf16[1280,1280]{1,0:T(8,128)(2,1)} %second_h.1, ...), custom_call_target="tpu_custom_call" | custom-call | flops 13421772800 | bytes 14680064 | tf_op jit(solution)/shard_map/pallas_call | solution.py:651
  77.6 3.2 %copy.13 = bf16[1,320,2,8,128]{4,3,2,1,0:T(8,128)(2,1)} copy(bf16[1,320,2,8,128]{4,1,3,2,0:T(8,128)(2,1)} %bitcast.9) | data formatting | bytes 2621440 | tf_op jit(solution)/shard_map/broadcast_in_dim | solution.py:696
  (2 shorter events, 0.0 us)

commit v4 on v3

--- a/solution.py
+++ b/solution.py
@@ -289,7 +289,14 @@
     mine = pl.ds(pl.multiple_of(step * own, 16), own)
     theirs = pl.ds(pl.multiple_of(partner * own, 16), own)
 
-    loads = [pltpu.make_async_copy(conv1_h, w1, wsem.at[0])]
+    loads = [
+        pltpu.make_async_copy(
+            conv1_h.at[t // 3, t % 3],
+            w1.at[pl.ds(t % 3 * chans, chans), pl.ds(t // 3 * 2 * chans, 2 * chans)],
+            wsem.at[t],
+        )
+        for t in range(9)
+    ]
     small = [
         pltpu.make_async_copy(src, dst, wsem.at[9 + i])
         for i, (src, dst) in enumerate(
@@ -397,6 +404,16 @@
         own_up().wait_recv()
         make_act(rows + 1, mine)
 
+    @pl.when(strip == 0)
+    def _():
+        act[0] = jnp.zeros(act.shape[1:], jnp.bfloat16)
+        act2[0] = jnp.zeros(act2.shape[1:], jnp.bfloat16)
+
+    @pl.when(strip == n_strip - 1)
+    def _():
+        act[rows + 1] = jnp.zeros(act.shape[1:], jnp.bfloat16)
+        act2[rows + 1] = jnp.zeros(act2.shape[1:], jnp.bfloat16)
+
     swap.wait()
     set_cols(slot_step[...], theirs)
 
@@ -417,77 +434,70 @@
     for load in loads:
         load.wait()
 
-    start_value = jnp.concatenate([emb[...], emb[...]], axis=1)
-
-    @pl.loop(0, rows + 4)
-    def _(r):
-        hid[r] = start_value
-
-    def add_taps(r, offsets):
-        image_row = act[r].reshape(2 * chans, 256)
-        for dy in offsets:
-            found = jnp.dot(
-                w1[dy].reshape(3 * chans, 2 * chans), image_row, preferred_element_type=jnp.float32
-            )
-            for f in range(2):
-                lanes = pl.ds(f * 128, 128)
-                hid[r - dy + 2, :, lanes] = hid[r - dy + 2, :, lanes] + join_taps(found, chans, f)
-
-    def add_skip(r):
-        skipped[r] = jnp.dot(
-            ws[...], raw[r + 1].reshape(2 * chans, 256), preferred_element_type=jnp.float32
-        )
-
-    def arrival(i):
-        later = (i + rows - 2) // rows
-        return (i - 1) * later + last * i * (1 - later)
-
-    @pl.loop(0, rows)
-    def _(i):
-        r = arrival(i)
-
-        @pl.when(i > 0)
-        def _():
-            add_skip(arrival(i - 1))
-
+    def arrive(r):
         row_copy(r).wait_recv()
 
-        @pl.when((i == 0) & has_up)
+        @pl.when((r == 0) & has_up)
         def _():
             far_up().start()
 
-        @pl.when((i == 1) & has_down)
+        @pl.when((r == last) & has_down)
         def _():
             far_down().start()
 
         make_act(r + 1, theirs)
-        add_taps(r + 1, (0, 1, 2))
-
-        @pl.when((i == rows - 3) & has_up)
-        def _():
-            far_down().wait_recv()
-            make_act(0, theirs)
-            add_taps(0, (0,))
-
-        @pl.when((i == rows - 3) & has_down)
-        def _():
-            far_up().wait_recv()
-            make_act(rows + 1, theirs)
-            add_taps(rows + 1, (2,))
+
+    def pair_dot(weights, first, second):
+        return jnp.dot(
+            weights[...], jnp.concatenate([first, second], axis=1), preferred_element_type=jnp.float32
+        )
 
     acc1[...] = jnp.zeros_like(acc1)
     acc2[...] = jnp.zeros_like(acc2)
 
-    @pl.loop(0, rows)
-    def _(c):
-        a, b = hid[c + 2, :, :128], hid[c + 2, :, 128:]
-        acc1[...] = acc1[...] + (a + b)
-        acc2[...] = acc2[...] + (a * a + b * b)
+    @pl.loop(0, 4)
+    def _(i):
+        later = (i + 2) // 4
+        arrive((i - 1) * later + last * i * (1 - later))
+
+    @pl.when(has_up)
+    def _():
+        far_down().wait_recv()
+        make_act(0, theirs)
+
+    @pl.when(has_down)
+    def _():
+        far_up().wait_recv()
+        make_act(rows + 1, theirs)
+
+    @pl.loop(0, rows // 2)
+    def _(i):
+        c = 2 * i
+
+        @pl.when((i > 0) & (i < rows // 2 - 1))
+        def _():
+            arrive(c + 1)
+            arrive(c + 2)
+
+        found = pair_dot(
+            w1, act[pl.ds(c, 3)].reshape(6 * chans, 256), act[pl.ds(c + 1, 3)].reshape(6 * chans, 256)
+        )
+        for k in range(2):
+            a, b = (join_taps(found, chans, 2 * k + f) + emb[...] for f in range(2))
+            hid[c + k, :, :128] = a
+            hid[c + k, :, 128:] = b
+            acc1[...] = acc1[...] + (a + b)
+            acc2[...] = acc2[...] + (a * a + b * b)
+
+        found = pair_dot(
+            ws, raw[c + 1].reshape(2 * chans, 256), raw[c + 2].reshape(2 * chans, 256)
+        )
+        skipped[c] = found[:, :256]
+        skipped[c + 1] = found[:, 256:]
 
     per_mid = chans // GROUPS
     stats[2] = pack_sums(acc1[...], acc2[...], per_mid)
     sent_mid = send_all(stats.at[2], slots.at[1], s_send.at[1], s_recv.at[1], peers)
-    add_skip(last - 1)
     total = add_all(stats.at[2], slots.at[1], sent_mid)
     mean, rstd = columns_of(total, chans, per_mid, float(entries * per_mid))
     cols_mid[0] = mean
@@ -496,7 +506,7 @@
     def mid_row(r):
         for f in range(2):
             lanes = pl.ds(f * 128, 128)
-            value = silu((hid[r + 2, :, lanes] - cols_mid[0]) * cols_mid[1])
+            value = silu((hid[r, :, lanes] - cols_mid[0]) * cols_mid[1])
             act2[r + 1, :, lanes] = value.astype(jnp.bfloat16)
 
     def mid_up():
@@ -529,74 +539,74 @@
         )
 
     def inner_first(i):
-        tail = i // (rows - 2)
-        return (i + 1) * (1 - tail) + (i - (rows - 2)) * last * tail
-
-    @pl.loop(0, rows)
+        tail = i // 2
+        return 2 * ((i + 1) * (1 - tail) + (i - 2) * (rows // 2 - 1) * tail)
+
+    @pl.loop(0, rows // 2)
     def _(i):
-        c = inner_first(i)
-
-        @pl.when((i == rows - 2) & has_up)
+        first = inner_first(i)
+
+        @pl.when((i == 2) & has_up)
         def _():
             mid_down().wait_recv()
 
-        @pl.when((i == rows - 2) & has_down)
+        @pl.when((i == 2) & has_down)
         def _():
             mid_up().wait_recv()
 
-        @pl.when((i == rows - 2) & (strip == 0))
-        def _():
-            act2[0] = jnp.zeros(act2.shape[1:], jnp.bfloat16)
-
-        @pl.when((i == rows - 2) & (strip == n_strip - 1))
-        def _():
-            act2[rows + 1] = jnp.zeros(act2.shape[1:], jnp.bfloat16)
-
-        window = act2[pl.ds(c, 3)].reshape(3 * chans, 256)
-        found = jnp.dot(w2[...], window, preferred_element_type=jnp.float32)
-        for f in range(2):
-            lanes = pl.ds(f * 128, 128)
-            second = join_taps(found, chans, f)
-            hid[c, :, lanes] = second
-            inner = silu(second).astype(jnp.bfloat16)
-            tbuf[c, 1, :, lanes] = inner
-            tbuf[c, 2 * f, :, pl.ds(128 - f * 128, 128)] = inner
-
-        @pl.when(has_prev)
-        def _():
-            to_prev(c).start()
-
-        @pl.when(has_next)
-        def _():
-            to_next(c).start()
-
-        @pl.when(frame == 0)
-        def _():
-            tbuf[c, 0, :, :128] = jnp.zeros((chans, 128), jnp.bfloat16)
-
-        @pl.when(frame == n_frame - 1)
-        def _():
-            tbuf[c, 2, :, 128:] = jnp.zeros((chans, 128), jnp.bfloat16)
-
-    @pl.loop(0, rows)
+        found = pair_dot(
+            w2,
+            act2[pl.ds(first, 3)].reshape(3 * chans, 256),
+            act2[pl.ds(first + 1, 3)].reshape(3 * chans, 256),
+        )
+        for k in range(2):
+            c = first + k
+            for f in range(2):
+                lanes = pl.ds(f * 128, 128)
+                second = join_taps(found, chans, 2 * k + f)
+                hid[c, :, lanes] = second
+                inner = silu(second).astype(jnp.bfloat16)
+                tbuf[c, 1, :, lanes] = inner
+                tbuf[c, 2 * f, :, pl.ds(128 - f * 128, 128)] = inner
+
+            @pl.when(has_prev)
+            def _():
+                to_prev(c).start()
+
+            @pl.when(has_next)
+            def _():
+                to_next(c).start()
+
+            @pl.when(frame == 0)
+            def _():
+                tbuf[c, 0, :, :128] = jnp.zeros((chans, 128), jnp.bfloat16)
+
+            @pl.when(frame == n_frame - 1)
+            def _():
+                tbuf[c, 2, :, 128:] = jnp.zeros((chans, 128), jnp.bfloat16)
+
+    @pl.loop(0, rows // 2)
     def _(i):
-        c = inner_first(i)
-        base = hid[c] + skipped[c]
-
-        @pl.when(has_prev)
-        def _():
-            to_next(c).wait_recv()
-
-        @pl.when(has_next)
-        def _():
-            to_prev(c).wait_recv()
-
-        mixed = jnp.dot(
-            wt[...], tbuf[c].reshape(3 * chans, 256), preferred_element_type=jnp.float32
-        )
-        result = (base + mixed).astype(jnp.bfloat16)
-        out[0, c] = result[:, :128]
-        out[1, c] = result[:, 128:]
+        first = inner_first(i)
+        for k in range(2):
+
+            @pl.when(has_prev)
+            def _():
+                to_next(first + k).wait_recv()
+
+            @pl.when(has_next)
+            def _():
+                to_prev(first + k).wait_recv()
+
+        mixed = pair_dot(
+            wt, tbuf[first].reshape(3 * chans, 256), tbuf[first + 1].reshape(3 * chans, 256)
+        )
+        for k in range(2):
+            c = first + k
+            result = mixed[:, 256 * k : 256 * k + 256] + (hid[c] + skipped[c])
+            result = result.astype(jnp.bfloat16)
+            out[0, c] = result[:, :128]
+            out[1, c] = result[:, 128:]
 
     @pl.loop(0, rows)
     def _(r):
@@ -656,7 +666,7 @@
         scratch_shapes=[
             pltpu.VMEM((rows + 2, 2, chans, width), bf16),
             pltpu.VMEM((rows + 2, 2, chans, width), bf16),
-            pltpu.VMEM((rows + 4, chans, width), f32),
+            pltpu.VMEM((rows, chans, width), f32),
             pltpu.VMEM((rows, chans, width), f32),
             pltpu.VMEM((rows + 2, chans, width), bf16),
             pltpu.VMEM((rows, 3, chans, width), bf16),
@@ -665,7 +675,7 @@
             pltpu.VMEM((2, 2, chans, 128), f32),
             pltpu.VMEM((2, chans, 128), f32),
             pltpu.VMEM((chans, 128), f32),
-            pltpu.VMEM((3, 3, chans, 2 * chans), bf16),
+            pltpu.VMEM((3 * chans, 6 * chans), bf16),
             pltpu.VMEM((3, 3, chans, chans), bf16),
             pltpu.VMEM((3 * chans, 3 * chans), bf16),
             pltpu.VMEM((3, chans, chans), bf16),

time: 81 us -> 81.9 us (1.011)
  Pallas kernels: 73.5 us -> 74.4 us
    pallas_call x1, Pallas kernels: 73.5 us -> 74.4 us  [in_kernel(): pl.pallas_call(functools.partial(block_kernel, (n_frame, n_strip)), out_s...]
where the time goes in v4:
time: 81.9 us; the launch traced here: 81.7 us
  Pallas kernels  74.4 us (91%)
  local copies, waits for them, and re-layouts  5.94 us (7%)
    pallas_call x1, Pallas kernels, in_kernel(): pl.pallas_call(functools.partial(block_kernel, (n_frame, n_strip)), out_s...  74.4 us
    broadcast_in_dim x1, local copies, waits for them, and re-layouts, in_kernel(): return result.transpose(2, 0, 1, 3)[None]  3.22 us
    transpose x1, local copies, waits for them, and re-layouts, in_kernel(): enc, skip = (part.transpose(1, 2, 0, 3) for part in (enc_feats, skip_feats))  2.71 us

profile of v4, /device:TPU:1, one launch (start us, length us, event | category | flops | bytes accessed | tf_op | source)
XLA Modules:
  0.0 81.7 jit_solution(74226782267715926)
XLA Ops:
  0.7 0.1 sine_convert_fusion
  0.7 0.6 pad_maximum_fusion.sinus
  1.4 2.7 %copy_bitcast_fusion = (bf16[2,8,160,128]{3,2,1,0:T(8,128)(2,1)}, bf16[2,8,160,128]{3,2,1,0:T(8,128)(2,1)}) fusion(bf16[160,2,8,128]{3,2,1,0:T(8,128)(2,1)} %param.11, bf16[160,2,8,128]{3,2,1,0:T(8,128)(2,1)} %param.10), kind=kLoop, calls=%fused_computation | loop fusion | bytes 2621440 | tf_op jit(solution)/shard_map/transpose | solution.py:648
  4.1 74.4 %shard_map.100 = bf16[2,8,320,128]{3,2,1,0:T(8,128)(2,1)} custom-call(bf16[2,8,160,128]{3,2,1,0:T(8,128)(2,1)} %get-tuple-element.8.enc, bf16[2,8,160,128]{3,2,1,0:T(8,128)(2,1)} %get-tuple-element.7.skip, bf16[1,320]{1,0:T(2,128)(2,1)} %pad_maximum_fusion.sinus, bf16[320,1280]{1,0:T(8,128)(2,1)} %first_h.1, bf16[1280,1280]{1,0:T(8,128)(2,1)} %second_h.1, ...), custom_call_target="tpu_custom_call" | custom-call | flops 13421772800 | bytes 14680064 | tf_op jit(solution)/shard_map/pallas_call | solution.py:661
  78.5 3.2 %copy.13 = bf16[1,320,2,8,128]{4,3,2,1,0:T(8,128)(2,1)} copy(bf16[1,320,2,8,128]{4,1,3,2,0:T(8,128)(2,1)} %bitcast.9) | data formatting | bytes 2621440 | tf_op jit(solution)/shard_map/broadcast_in_dim | solution.py:706
  (2 shorter events, 0.0 us)
